TPU v7x, 256 devices: a whole 4x4x8 slice. The times are simulated.
256 devices in a mesh: tilt: 64 (over x, z, core), slab: 4 (over y).
Axes of the slice: x: 4, y: 4, z: 8, core: 2. Of those that a mesh axis runs over, the one named last changes fastest.
Arguments:
- tilt_images: bfloat16 [64, 256, 256], P('tilt'), may hold values from -68 to 68
- corners: int32 [2, 64, 128], P(None, 'tilt'), may hold values from 0 to 128
- visible: int32 [64, 128], P('tilt'), may hold values 0 or 1
- defocus: float32 [128, 64], P('tilt'), may hold values from 5 to 40
- labels: int32 [128], P('tilt'), may hold values from 0 to 3
- row_owner: int32 [128, 64, 128, 1], P('tilt'), may hold values from 0 to 255; in each aligned block of 16384 rows (0 to 16383, 16384 to 32767, ..., all dimensions but the last counted through in order) at most 128 rows name the same one
- row_offset: int32 [128, 64, 128], P('tilt'), may hold values from 0 to 63
Outputs:
- class_maps: float32 [2, 4, 16384, 128], P(None, None, ('tilt', 'slab'))
Inputs may be any that keep to these rules, and one draw needn't show every extreme that they name: `row_owner`: among the slice rows of the particles of one index of tilt, at most 128 fall in one block, and some block receives exactly 128.
All inputs are finite; a program needn't handle non-finite values. No bound on the sum of `visible` on one device may be relied on, other than what follows from the above.
Results may differ from a plain program's by a relative error of at most 0.007.
Values may be sent and summed in bfloat16 or wider, within the bound.
A program may use at most 128 MiB of HBM per device.

v0:
```python
import jax
import jax.numpy as jnp
from jax import lax
from jax.sharding import PartitionSpec as P

BOX = 128
HALFMAPS = 4


AMPLITUDE = 0.1


def fourier_tables(width):
    positions = jnp.arange(width, dtype=jnp.int32)
    frequency = positions - width // 2
    phase_index = frequency[:, None] * positions[None, :] % width
    angles = phase_index.astype(jnp.float32) * (2.0 * jnp.pi / width)
    return (jnp.cos(angles).astype(jnp.bfloat16), (-jnp.sin(angles)).astype(jnp.bfloat16))


def contrast_transfer(defocus_values, width):
    frequency = (jnp.arange(width, dtype=jnp.int32) - width // 2).astype(jnp.float32) / width
    radius_sq = frequency[:, None] ** 2 + frequency[None, :] ** 2
    aberration = jnp.pi * defocus_values[..., None, None] * radius_sq
    return -(
        jnp.sqrt(1.0 - AMPLITUDE * AMPLITUDE) * jnp.sin(aberration)
        + AMPLITUDE * jnp.cos(aberration)
    )


def normalize(patches, seen_mask):
    values = patches.astype(jnp.float32)
    average = jnp.mean(values, axis=(-2, -1), keepdims=True)
    centered = values - average
    variance = jnp.mean(centered * centered, axis=(-2, -1), keepdims=True)
    scaled = centered * lax.rsqrt(variance + 1e-05) * seen_mask.astype(jnp.float32)[..., None, None]
    return scaled.astype(jnp.bfloat16)


def cut_windows(micrograph, corner_rows, corner_cols):
    image_side = micrograph.shape[0]
    window = jnp.arange(BOX, dtype=jnp.int32)
    pixels = jnp.arange(image_side, dtype=jnp.int32)
    row_pick = ((corner_rows[..., None] + window)[..., None] == pixels).astype(jnp.bfloat16)
    col_pick = ((corner_cols[..., None] + window)[..., None] == pixels).astype(jnp.bfloat16)
    band = jnp.einsum(
        "ptki,ij->ptkj", row_pick, micrograph, preferred_element_type=jnp.float32
    ).astype(jnp.bfloat16)
    return jnp.einsum("ptkj,ptlj->ptkl", band, col_pick, preferred_element_type=jnp.float32).astype(
        jnp.bfloat16
    )


def body(tilt_images, corners, visible, defocus, labels, row_owner, row_offset):
    tilt_count = lax.axis_size("tilt")
    slab_count = lax.axis_size("slab")
    slab_index = lax.axis_index("slab")
    part_dev = labels.shape[0]
    micrograph = tilt_images[0]
    corner_rows = corners[0, 0].reshape(tilt_count, part_dev).T
    corner_cols = corners[1, 0].reshape(tilt_count, part_dev).T
    seen_mask = visible[0].reshape(tilt_count, part_dev).T
    patches = normalize(cut_windows(micrograph, corner_rows, corner_cols), seen_mask)
    cos_table, sin_table = fourier_tables(BOX)
    stacked = jnp.concatenate([cos_table, sin_table], 0)
    first_section = jnp.einsum(
        "kn,ptnm->ptkm",
        stacked,
        lax.all_to_all(patches, "tilt", split_axis=1, concat_axis=1, tiled=True),
        preferred_element_type=jnp.float32,
    ).astype(jnp.bfloat16)
    second = jnp.einsum("ptkm,lm->ptkl", first_section, stacked, preferred_element_type=jnp.float32)
    real_part = second[..., :BOX, :BOX] - second[..., BOX:, BOX:]
    imag_part = second[..., :BOX, BOX:] + second[..., BOX:, :BOX]
    transfer = contrast_transfer(defocus, BOX)
    slice_real = (transfer * real_part / BOX).astype(jnp.bfloat16)
    slice_imag = (transfer * imag_part / BOX).astype(jnp.bfloat16)
    height = BOX * BOX // (tilt_count * slab_count)
    owner = row_owner[..., 0]
    owner_slab = owner % slab_count
    owner_tilt = owner // slab_count
    kept = owner_slab == slab_index
    map_cells = tilt_count * height
    cell_count = HALFMAPS * map_cells
    segment_ids = jnp.where(
        kept, labels[:, None, None] * map_cells + owner_tilt * height + row_offset, cell_count
    ).reshape(-1)
    real_sum = jax.ops.segment_sum(
        slice_real.reshape(-1, BOX).astype(jnp.float32), segment_ids, num_segments=cell_count + 1
    )
    imag_sum = jax.ops.segment_sum(
        slice_imag.reshape(-1, BOX).astype(jnp.float32), segment_ids, num_segments=cell_count + 1
    )
    partial_value = jnp.stack([real_sum[:cell_count], imag_sum[:cell_count]])
    partial_value = partial_value.reshape(2, HALFMAPS, map_cells, BOX)
    own_rows = lax.psum_scatter(partial_value, "tilt", scatter_dimension=2, tiled=True)
    return own_rows


def solution(mesh):
    return jax.shard_map(
        body,
        mesh=mesh,
        in_specs=(
            P("tilt", None, None),
            P(None, "tilt", None),
            P("tilt", None),
            P("tilt", None),
            P("tilt"),
            P("tilt", None, None, None),
            P("tilt", None, None),
        ),
        out_specs=P(None, None, ("tilt", "slab"), None),
        check_vma=False,
    )
```

profile of v0, /device:TPU:8, one launch (start us, length us, event | category | flops | bytes accessed | tf_op | source)
XLA Modules:
  0.0 586.9 jit_solution(631165736943351591)
XLA Ops:
  6.5 0.7 slice_reduce_fusion.1
  7.3 0.1 reshape_squeeze.7
  7.4 0.1 copy.14
  7.5 0.1 reshape_squeeze.8
  7.6 0.1 copy.15
  7.7 0.1 iota_add_fusion
  7.8 4.1 fusion.35.clone.5
  11.9 0.0 copy-start.6
  11.9 5.9 convert_reduce_fusion
  17.8 1.9 copy-done.2
  19.7 1.8 fusion.4
  21.5 0.1 convert_element_type.74
  21.6 0.1 copy.16
  21.7 3.5 fusion.6
  25.2 0.0 copy-start.7
  25.2 0.0 copy-start.5
  25.2 2.2 copy.17
  27.5 12.2 %all-to-all-start = ((bf16[2,64,128,128]{3,2,0,1:T(8,128)(2,1)}), bf16[2,64,128,128]{3,2,0,1:T(8,128)(2,1)}, u32[]{:S(2)}, u32[]{:S(2)}) async-start(bf16[2,64,128,128]{3,2,0,1:T(8,128)(2,1)} %copy.17), calls=%async_computation | async-start | bytes 8388608 | tf_op jit(solution)/shard_map/all_to_all | solution.py:69
  39.7 0.2 reduce-scatter.2.cloned.1.call-start
  40.0 0.3 cosine_convert_fusion
  40.3 0.1 broadcast_add_fusion
  40.4 0.1 fusion.42
  40.5 94.9 %all-to-all-done = bf16[2,64,128,128]{3,2,0,1:T(8,128)(2,1)} async-done(((bf16[2,64,128,128]{3,2,0,1:T(8,128)(2,1)}), bf16[2,64,128,128]{3,2,0,1:T(8,128)(2,1)}, u32[]{:S(2)}, u32[]{:S(2)}) %all-to-all-start) | async-done | bytes 4194336 | tf_op jit(solution)/shard_map/all_to_all | solution.py:69
  135.4 16.5 %fusion.21 = f32[2,64,256,256]{3,2,1,0:T(8,128)} fusion(bf16[2,64,128,128]{3,2,0,1:T(8,128)(2,1)} %all-to-all-done, bf16[128,128]{1,0:T(8,128)(2,1)S(1)} %get-tuple-element.10, bf16[128,128]{1,0:T(8,128)(2,1)S(1)} %get-tuple-element.9), kind=kOutput, calls=%fused_computation.32 | convolution fusion | flops 3225681920 | bytes 37814272 | tf_op jit(solution)/shard_map/ptkm,lm->ptkl/dot_general | solution.py:72
  151.9 38.6 %fusion.14 = (bf16[2,64,128,128]{3,2,1,0:T(8,128)(2,1)}, bf16[2,64,128,128]{3,2,1,0:T(8,128)(2,1)}) fusion(f32[2,64,256,256]{3,2,1,0:T(8,128)} %fusion.21, f32[128,128]{1,0:T(8,128)S(1)} %broadcast_add_fusion, f32[2,64]{1,0:T(2,128)S(1)} %broadcast_multiply_fusion.1), kind=kLoop, calls=%fused_computation.23 | loop fusion | flops 27262976 | bytes 42009088 | tf_op jit(solution)/shard_map/convert_element_type | solution.py:76
  190.5 93.3 %scatter_custom_fusion = f32[16385,128]{1,0:T(8,128)} fusion(s32[16384]{0:T(1024)S(1)} %bitcast.43, bf16[16384,128]{1,0:T(8,128)(2,1)} %bitcast.38, f32[]{:T(128)} %constant.57.clone.1), kind=kCustom, calls=%fused_computation.30 | custom fusion | flops 4194304 | bytes 12583428 | tf_op jit(solution)/shard_map/scatter-add | solution.py:88
  283.8 93.3 %scatter_custom_fusion.1 = f32[16385,128]{1,0:T(8,128)} fusion(s32[16384]{0:T(1024)S(1)} %bitcast.44, bf16[16384,128]{1,0:T(8,128)(2,1)} %bitcast.37, f32[]{:T(128)} %constant.57.clone.1), kind=kCustom, calls=%fused_computation.28 | custom fusion | flops 4194304 | bytes 12583428 | tf_op jit(solution)/shard_map/scatter-add | solution.py:91
  377.1 3.4 slice-done
  380.5 2.4 slice-done.1
  382.8 6.0 %pad_maximum_fusion = f32[2,4,4096,128]{3,2,1,0:T(8,128)} fusion(f32[1,4,4096,128]{3,2,1,0:T(8,128)S(1)} %bitcast.35, f32[1,4,4096,128]{3,2,1,0:T(8,128)S(1)} %bitcast.36), kind=kLoop, calls=%fused_computation.2 | loop fusion | flops 4194304 | bytes 33554432 | tf_op jit(solution)/shard_map/stack | solution.py:94
  388.8 0.0 reduce-scatter.2.cloned.1.call-update
  388.9 191.2 %reduce-scatter.2.cloned.1.call-done = f32[2,4,64,128]{3,2,1,0:T(8,128)} async-done(((f32[2,4,4096,128]{3,2,1,0:T(8,128)}), f32[2,4,64,128]{3,2,1,0:T(8,128)}) %reduce-scatter.2.cloned.1.call-update) | async-done | bytes 262160 | tf_op jit(solution)/shard_map/reduce_scatter | solution.py:96
  (21 shorter events, 0.1 us)
Async XLA Ops:
  6.5 1.3 copy-start
  11.9 9.6 %copy-start.6 = (s32[1,128]{1,0:T(1,128)S(1)}, s32[1,128]{1,0:T(1,128)}, u32[]{:S(2)}) copy-start(s32[1,128]{1,0:T(1,128)} %param.9) | copy-start | bytes 1540
  17.8 1.9 copy-start.2
  25.2 14.7 %copy-start.7 = (s32[2]{0:T(128)S(1)}, s32[2]{0:T(128)}, u32[]{:S(2)}) copy-start(s32[2]{0:T(128)} %param.11) | copy-start | bytes 28
  25.2 14.8 %copy-start.5 = (f32[2,64]{1,0:T(2,128)S(1)}, f32[2,64]{1,0:T(2,128)}, u32[]{:S(2)}) copy-start(f32[2,64]{1,0:T(2,128)} %param.10) | copy-start | bytes 1540
  25.2 15.2 %copy-start.3 = (s32[2,64,128]{2,1,0:T(8,128)S(1)}, s32[2,64,128]{2,1,0:T(8,128)}, u32[]{:S(2)}) copy-start(s32[2,64,128]{2,1,0:T(8,128)} %param.13) | copy-start | bytes 196612
  25.2 15.2 %copy-start.4 = (s32[2,64,128,1]{2,3,1,0:T(1,128)S(1)}, s32[2,64,128,1]{2,3,1,0:T(1,128)}, u32[]{:S(2)}) copy-start(s32[2,64,128,1]{2,3,1,0:T(1,128)} %param.12) | copy-start | bytes 196612
  27.5 107.9 %all-to-all-start = ((bf16[2,64,128,128]{3,2,0,1:T(8,128)(2,1)}), bf16[2,64,128,128]{3,2,0,1:T(8,128)(2,1)}, u32[]{:S(2)}, u32[]{:S(2)}) async-start(bf16[2,64,128,128]{3,2,0,1:T(8,128)(2,1)} %copy.17), calls=%async_computation | async-start | bytes 8388608 | tf_op jit(solution)/shard_map/all_to_all | solution.py:69
  39.7 540.3 %reduce-scatter.2.cloned.1.call-start = ((), (), s32[]{:S(2)}) async-start(), calls=%async_computation.2 | async-start | bytes 17039360 | tf_op jit(solution)/shard_map/reduce_scatter | solution.py:96
  377.1 3.4 slice-start
  377.1 5.8 slice-start.1
  388.8 191.2 %copy-start.1 = (bf16[1,256,256]{2,1,0:T(8,128)(2,1)S(1)}, bf16[1,256,256]{2,1,0:T(8,128)(2,1)}, u32[]{:S(2)}) copy-start(bf16[1,256,256]{2,1,0:T(8,128)(2,1)} %param.7) | copy-start | bytes 393220
Sparse Core Ops, SparseCore 0:
  389.0 191.0 reduce-scatter.1
where the time goes:
time: 587 us
  waiting for transfers between devices  286 us (49%)
  other arithmetic  237 us (40%)
  matrix products  26.5 us (5%)
  between operations  13.6 us (2%)
  starting transfers between devices  12.4 us (2%)
  local copies, waits for them, and re-layouts  11.3 us (2%)
    reduce_scatter x1, waiting for transfers between devices, body(): lax.psum_scatter(partial_value, 'tilt', scatter_dimension=2, tiled=True)  191 us
    all_to_all x1, waiting for transfers between devices, body(): lax.all_to_all(patches, 'tilt', split_axis=1, concat_axis=1, tiled=True)  94.9 us
    scatter-add x1, other arithmetic, body(): jax.ops.segment_sum(slice_real.reshape(-1, BOX).astype(jnp.float32), segm...  93.3 us
    scatter-add x1, other arithmetic, body(): jax.ops.segment_sum(slice_imag.reshape(-1, BOX).astype(jnp.float32), segm...  93.3 us
    convert_element_type x1, other arithmetic, body(): slice_real = (transfer * real_part / BOX).astype(jnp.bfloat16)  38.6 us
    dot_general x1, matrix products, body(): jnp.einsum('ptkm,lm->ptkl', first_section, stacked, preferred_element_typ...  16.5 us
    all_to_all x1, starting transfers between devices, body(): lax.all_to_all(patches, 'tilt', split_axis=1, concat_axis=1, tiled=True)  12.2 us
  transfers between devices with their start and end apart: 2, of which 2 were waited for; matrix products, arithmetic and copies ran while one was open for 0% of the time, Pallas kernels for 0%

commit v1 on v0

v1 whole, which is shorter than its diff:
```python
import jax
import jax.numpy as jnp
import numpy as np
from jax import lax
from jax.experimental import pallas as pl
from jax.experimental.pallas import tpu as pltpu
from jax.sharding import PartitionSpec as P

BOX = 128
HALFMAPS = 4
AMPLITUDE = 0.1
TILTS = 64
PARTICLES = 128
CELLS = TILTS * HALFMAPS * 64
GROUP = 16
WINDOW = 2 * GROUP


def fourier_tables(width):
    positions = jnp.arange(width, dtype=jnp.int32)
    frequency = positions - width // 2
    phase_index = frequency[:, None] * positions[None, :] % width
    angles = phase_index.astype(jnp.float32) * (2.0 * jnp.pi / width)
    return (jnp.cos(angles).astype(jnp.bfloat16), (-jnp.sin(angles)).astype(jnp.bfloat16))


def transfer_factors(defocus_values):
    frequency = (jnp.arange(BOX, dtype=jnp.int32) - BOX // 2).astype(jnp.float32) / BOX
    angle = jnp.pi * defocus_values[:, None] * (frequency * frequency)[None, :]
    cos_part, sin_part = jnp.cos(angle), jnp.sin(angle)
    main = jnp.sqrt(1.0 - AMPLITUDE * AMPLITUDE)
    first = -(main * sin_part + AMPLITUDE * cos_part) / BOX
    second = -(main * cos_part - AMPLITUDE * sin_part) / BOX
    return first.T, second.T, cos_part, sin_part


def insert_kernel(corner_ref, seen_ref, image_ref, places_ref, stacked_ref, mixed_ref, first_ref, second_ref,
                  cos_ref, sin_ref, out_ref, left, right, main_list, late_list, late_any, main_s, late_s, any_s,
                  slices_a, slices_b, table, sems):
    lane = lax.broadcasted_iota(jnp.int32, (BOX, BOX), 1)
    dump = 2 * CELLS + 2 * (lane % GROUP)
    places = places_ref[...]
    kept = places >= 0
    later = jnp.zeros((BOX, BOX), jnp.bool_)
    for d in range(1, WINDOW):
        other = pltpu.roll(places, BOX - d, axis=1)
        later = later | ((other == places) & (lane < BOX - d))
    late = later & kept
    main_list[...] = jnp.where(kept & ~late, places, dump)
    late_list[...] = jnp.where(late, places, dump)
    late_any[...] = jnp.broadcast_to(
        jnp.max(jnp.where(late, 1, 0), axis=1, keepdims=True), (BOX, BOX))
    copies = [
        pltpu.make_async_copy(main_list, main_s, sems.at[0]),
        pltpu.make_async_copy(late_list, late_s, sems.at[1]),
        pltpu.make_async_copy(late_any, any_s, sems.at[2]),
    ]
    for copy in copies:
        copy.start()
    left[...] = image_ref[:, :BOX].astype(jnp.float32)
    right[...] = image_ref[:, BOX:].astype(jnp.float32)

    def clear(i, carry):
        table[pl.ds(pl.multiple_of(i * 512, 512), 512), :] = jnp.zeros((512, BOX), jnp.float32)
        return carry

    lax.fori_loop(0, 2 * CELLS // 512, clear, 0)
    for copy in copies:
        copy.wait()

    def window(p):
        row, col = corner_ref[0, p], corner_ref[1, p]
        a = left[pl.ds(row, BOX), :]
        b = right[pl.ds(row, BOX), :]
        cut = pltpu.roll(jnp.where(lane >= col, a, b), (BOX - col) % BOX, axis=1)
        average = jnp.sum(jnp.sum(cut, axis=0, keepdims=True), axis=1, keepdims=True) * (1.0 / (BOX * BOX))
        centered = cut - average
        variance = jnp.sum(
            jnp.sum(centered * centered, axis=0, keepdims=True), axis=1, keepdims=True) * (1.0 / (BOX * BOX))
        scale = lax.rsqrt(variance + 1e-05) * seen_ref[0, p].astype(jnp.float32)
        return (centered * scale).astype(jnp.bfloat16)

    def slices_of(pair):
        p = 2 * pair
        patches = jnp.concatenate([window(p), window(p + 1)], axis=1)
        section = jnp.dot(stacked_ref[...], patches, preferred_element_type=jnp.float32).astype(jnp.bfloat16)
        for j, target in ((0, slices_a), (1, slices_b)):
            side = jnp.concatenate(
                [section[:BOX, j * BOX:(j + 1) * BOX], section[BOX:, j * BOX:(j + 1) * BOX]], axis=1)
            spectrum = jnp.dot(side, mixed_ref[...], preferred_element_type=jnp.float32)
            pick = jnp.full((BOX, BOX), p + j, jnp.int32)
            first = jnp.take_along_axis(first_ref[...], pick, axis=1)
            second = jnp.take_along_axis(second_ref[...], pick, axis=1)
            transfer = first * cos_ref[pl.ds(p + j, 1), :] + second * sin_ref[pl.ds(p + j, 1), :]
            target[pl.ds(0, BOX, stride=2), :] = transfer * spectrum[:, :BOX]
            target[pl.ds(1, BOX, stride=2), :] = transfer * spectrum[:, BOX:]

    def insert(p, source):
        waiting = None
        for g in range(BOX // GROUP + 1):
            if g < BOX // GROUP:
                spots = [main_s[p, g * GROUP + i] for i in range(GROUP)]
                sums = [table[pl.ds(spots[i], 2), :] + source[pl.ds(2 * (g * GROUP + i), 2), :]
                        for i in range(GROUP)]
            if waiting is not None:
                for spot, total in zip(*waiting):
                    table[pl.ds(spot, 2), :] = total
            waiting = (spots, sums)

        @pl.when(any_s[p, 0] > 0)
        def _():
            def one(i, carry):
                spot = late_s[p, i]
                table[pl.ds(spot, 2), :] += source[pl.ds(2 * i, 2), :]
                return carry

            lax.fori_loop(0, BOX, one, 0)

    def step(pair, carry):
        slices_of(pair)
        insert(2 * pair, slices_a)
        insert(2 * pair + 1, slices_b)
        return carry

    lax.fori_loop(0, PARTICLES // 2, step, 0)

    def finish(i, carry):
        rows = pl.ds(pl.multiple_of(i * 512, 512), 512)
        out_ref[rows, :] = table[rows, :].astype(jnp.bfloat16)
        return carry

    lax.fori_loop(0, 2 * CELLS // 512, finish, 0)


def insert(corners, seen, image, places, stacked, mixed, factors):
    whole = pl.BlockSpec(memory_space=pltpu.VMEM)
    scalars = pl.BlockSpec(memory_space=pltpu.SMEM)
    return pl.pallas_call(
        insert_kernel,
        out_shape=jax.ShapeDtypeStruct((2 * CELLS, BOX), jnp.bfloat16),
        in_specs=[scalars, scalars] + [whole] * 8,
        out_specs=whole,
        scratch_shapes=[
            pltpu.VMEM((256, BOX), jnp.float32),
            pltpu.VMEM((256, BOX), jnp.float32),
            pltpu.VMEM((BOX, BOX), jnp.int32),
            pltpu.VMEM((BOX, BOX), jnp.int32),
            pltpu.VMEM((BOX, BOX), jnp.int32),
            pltpu.SMEM((BOX, BOX), jnp.int32),
            pltpu.SMEM((BOX, BOX), jnp.int32),
            pltpu.SMEM((BOX, BOX), jnp.int32),
            pltpu.VMEM((2 * BOX, BOX), jnp.float32),
            pltpu.VMEM((2 * BOX, BOX), jnp.float32),
            pltpu.VMEM((2 * CELLS + 2 * GROUP, BOX), jnp.float32),
            pltpu.SemaphoreType.DMA((3,)),
        ],
        compiler_params=pltpu.CompilerParams(vmem_limit_bytes=48 * 2**20),
        name="insert_slices",
    )(corners, seen, image, places, stacked, mixed, *factors)


def tables():
    cos_table, sin_table = fourier_tables(BOX)
    stacked = jnp.concatenate([cos_table, sin_table], 0)
    mixed = jnp.concatenate([
        jnp.concatenate([cos_table.T, sin_table.T], 1),
        jnp.concatenate([-sin_table.T, cos_table.T], 1)], 0)
    return stacked, mixed


def places_of(rows, labels, slab_index, slab_count):
    owner, offset = rows // 64, rows % 64
    owner_tilt = owner // slab_count
    block = (owner_tilt % 2) * (TILTS // 2) + owner_tilt // 2
    place = 2 * ((block * HALFMAPS + labels[:, None]) * 64 + offset)
    return jnp.where(owner % slab_count == slab_index, place, -1 - lax.broadcasted_iota(jnp.int32, rows.shape, 1))


def body(tilt_images, corners, visible, defocus, labels, row_owner, row_offset):
    slab_count = lax.axis_size("slab")
    slab_index = lax.axis_index("slab")
    rows = (row_owner[..., 0] * 64 + row_offset).astype(jnp.float32)
    packed = jnp.concatenate([
        rows.transpose(1, 0, 2),
        jnp.pad(jnp.stack([defocus.T, jnp.broadcast_to(labels.astype(jnp.float32), (TILTS, 2))], 1),
                ((0, 0), (0, 0), (0, BOX - 2)))], 1)
    packed = lax.all_to_all(packed, "tilt", split_axis=0, concat_axis=0, tiled=True)
    rows = packed[:, :2].reshape(PARTICLES, BOX).astype(jnp.int32)
    defocus_all = packed[:, 2, :2].reshape(PARTICLES)
    labels_all = packed[:, 3, :2].reshape(PARTICLES).astype(jnp.int32)
    places = places_of(rows, labels_all, slab_index, slab_count)
    stacked, mixed = tables()
    table = insert(corners[:, 0], visible, tilt_images[0], places, stacked, mixed, transfer_factors(defocus_all))
    table = table.reshape(2, 4, 8, HALFMAPS, 64, 2, BOX).transpose(1, 2, 0, 3, 4, 5, 6).reshape(TILTS, -1, BOX)
    own = lax.psum_scatter(table, "tilt", scatter_dimension=0, tiled=True)
    own = own.reshape(HALFMAPS, 64, 2, BOX)
    return own.transpose(2, 0, 1, 3).astype(jnp.float32)


def solution(mesh):
    return jax.shard_map(
        body,
        mesh=mesh,
        in_specs=(
            P("tilt", None, None),
            P(None, "tilt", None),
            P("tilt", None),
            P("tilt", None),
            P("tilt"),
            P("tilt", None, None, None),
            P("tilt", None, None),
        ),
        out_specs=P(None, None, ("tilt", "slab"), None),
        check_vma=False,
    )
```

time: 587 us -> 295 us (0.50)
  other arithmetic: 237 us -> 4.18 us
  waiting for transfers between devices: 286 us -> 158 us
  Pallas kernels: 0 us -> 92.9 us
  matrix products: 26.5 us -> 0 us
    scatter-add x2 -> x0, other arithmetic: 187 us -> none  [the longest x1 93.3 us: body(): jax.ops.segment_sum(slice_real.reshape(-1, BOX).astype(jnp.float32), segm...]
    pallas_call x0 -> x1, Pallas kernels: none -> 92.9 us  [insert(): pl.pallas_call(insert_kernel, out_shape=jax.ShapeDtypeStruct((2 * CELLS,...]
    all_to_all x1, waiting for transfers between devices: 94.9 us -> 9.34 us  [body(): lax.all_to_all(packed, 'tilt', split_axis=0, concat_axis=0, tiled=True)]
    reduce_scatter x1, waiting for transfers between devices: 191 us -> 148 us  [body(): own = lax.psum_scatter(table, 'tilt', scatter_dimension=0, tiled=True)]
    convert_element_type x4, other arithmetic: 42.5 us -> 1.36 us  [the longest x1 0.66 us: body(): labels.astype(jnp.float32)]
    dot_general x3 -> x0, matrix products: 26.5 us -> none  [the longest x1 16.5 us: body(): jnp.einsum('ptkm,lm->ptkl', first_section, stacked, preferred_element_typ...]
    reshape x0 -> x1, local copies, waits for them, and re-layouts: none -> 8.58 us  [body(): table.reshape(2, 4, 8, HALFMAPS, 64, 2, BOX).transpose(1, 2, 0, 3, 4, 5, 6)]
    slice x5 -> x0, local copies, waits for them, and re-layouts: 6.49 us -> none  [the longest x4 5.77 us: body(): partial_value = jnp.stack([real_sum[:cell_count], imag_sum[:cell_count]])]
where the time goes in v1:
time: 295 us
  waiting for transfers between devices  158 us (54%)
  Pallas kernels  92.9 us (31%)
  local copies, waits for them, and re-layouts  14.5 us (5%)
  between operations  13.5 us (5%)
  starting transfers between devices  12 us (4%)
  other arithmetic  4.18 us (1%)
    reduce_scatter x1, waiting for transfers between devices, body(): own = lax.psum_scatter(table, 'tilt', scatter_dimension=0, tiled=True)  148 us
    pallas_call x1, Pallas kernels, insert(): pl.pallas_call(insert_kernel, out_shape=jax.ShapeDtypeStruct((2 * CELLS,...  92.9 us
    all_to_all x1, starting transfers between devices, body(): lax.all_to_all(packed, 'tilt', split_axis=0, concat_axis=0, tiled=True)  11.9 us
    all_to_all x1, waiting for transfers between devices, body(): lax.all_to_all(packed, 'tilt', split_axis=0, concat_axis=0, tiled=True)  9.34 us
    reshape x1, local copies, waits for them, and re-layouts, body(): table.reshape(2, 4, 8, HALFMAPS, 64, 2, BOX).transpose(1, 2, 0, 3, 4, 5, 6)  8.58 us
  transfers between devices with their start and end apart: 2, of which 2 were waited for; matrix products, arithmetic and copies ran while one was open for 0% of the time, Pallas kernels for 0%

profile of v1, /device:TPU:8, one launch (start us, length us, event | category | flops | bytes accessed | tf_op | source)
XLA Modules:
  0.0 294.9 jit_solution(5509439332238291208)
XLA Ops:
  6.5 0.7 convert_element_type.74
  7.2 0.9 copy.20
  8.1 0.9 copy.21
  9.1 0.1 stack_broadcast_in_dim.3
  9.1 0.7 select_maximum_fusion
  9.9 0.8 copy.22
  10.7 11.9 %all-to-all-start = ((f32[64,4,128]{2,1,0:T(4,128)}), f32[64,4,128]{2,1,0:T(4,128)S(1)}, u32[]{:S(2)}, u32[]{:S(2)}) async-start(f32[64,4,128]{2,1,0:T(4,128)} %copy.22), calls=%async_computation | async-start | bytes 262144 | tf_op jit(solution)/shard_map/all_to_all | solution.py:187
  22.6 0.0 reduce-scatter.2.cloned.1.call-start
  22.7 0.3 fusion.42
  22.9 0.6 negate_convert_fusion
  23.6 9.3 %all-to-all-done = f32[64,4,128]{2,1,0:T(4,128)S(1)} async-done(((f32[64,4,128]{2,1,0:T(4,128)}), f32[64,4,128]{2,1,0:T(4,128)S(1)}, u32[]{:S(2)}, u32[]{:S(2)}) %all-to-all-start) | async-done | bytes 131104 | tf_op jit(solution)/shard_map/all_to_all | solution.py:187
  32.9 0.1 fusion.40
  33.0 0.1 mul.169
  33.2 0.1 fusion.41
  33.3 0.1 convert_element_type.78
  33.4 0.6 multiply_sine_fusion
  34.0 0.2 fusion.20.places_ref
  34.2 0.0 copy-start
  34.2 0.9 copy-done
  35.1 0.0 copy-start.1
  35.1 0.7 copy-done.1
  35.8 0.0 copy-start.2
  35.8 0.7 copy-done.2
  36.5 92.9 %insert_slices.1 = bf16[32768,128]{1,0:T(8,128)(2,1)} custom-call(s32[2,128]{1,0:T(2,128)S(1)} %bitcast.25, s32[1,128]{1,0:T(1,128)S(1)} %copy-done.2, bf16[256,256]{1,0:T(8,128)(2,1)S(1)} %bitcast.24, s32[128,128]{1,0:T(8,128)S(1)} %fusion.20.places_ref, bf16[256,128]{1,0:T(8,128)(2,1)S(1)} %pad_maximum_fusion.1.stacked_ref, ...), custom_call_target="tpu_custom_call" | custom-call | tf_op jit(solution)/shard_map/insert_slices/pallas_call | solution.py:138
  129.4 8.6 %copy.23 = bf16[2,4,8,4,64,2,128]{6,5,4,3,0,2,1:T(2,128)(2,1)} copy(bf16[2,4,8,4,64,2,128]{6,5,4,3,2,1,0:T(2,128)(2,1)} %bitcast.27) | data formatting | bytes 16777216 | tf_op jit(solution)/shard_map/reshape | solution.py:194
  138.0 0.0 reduce-scatter.2.cloned.1.call-update
  138.0 148.4 %reduce-scatter.2.cloned.1.call-done = bf16[1,512,128]{2,1,0:T(8,128)(2,1)} async-done(((bf16[64,512,128]{2,1,0:T(8,128)(2,1)}), bf16[1,512,128]{2,1,0:T(8,128)(2,1)}) %reduce-scatter.2.cloned.1.call-update) | async-done | bytes 131088 | tf_op jit(solution)/shard_map/reduce_scatter | solution.py:195
  286.4 0.9 convert.5
  287.3 0.7 copy.24
  (8 shorter events, 0.1 us)
Async XLA Ops:
  10.7 22.2 %all-to-all-start = ((f32[64,4,128]{2,1,0:T(4,128)}), f32[64,4,128]{2,1,0:T(4,128)S(1)}, u32[]{:S(2)}, u32[]{:S(2)}) async-start(f32[64,4,128]{2,1,0:T(4,128)} %copy.22), calls=%async_computation | async-start | bytes 262144 | tf_op jit(solution)/shard_map/all_to_all | solution.py:187
  22.6 263.8 %reduce-scatter.2.cloned.1.call-start = ((), (), s32[]{:S(2)}) async-start(), calls=%async_computation.2 | async-start | bytes 8519680 | tf_op jit(solution)/shard_map/reduce_scatter | solution.py:195
  34.2 0.9 copy-start
  35.1 0.7 copy-start.1
  35.8 0.7 copy-start.2
Sparse Core Ops, SparseCore 0:
  138.1 148.2 reduce-scatter.1

commit v2 on v1

--- a/solution.py
+++ b/solution.py
@@ -159,6 +159,208 @@
     )(corners, seen, image, places, stacked, mixed, *factors)
 
 
+ZS, XS = 8, 4
+PART_ROWS = TILTS // 2 * BOX
+SPOTS = 2 * CELLS
+
+
+def reduce_kernel(table_ref, out_ref, own, sib, send_a, recv_a, send_b, recv_b, mid_a, mid_b, send_c, recv_c, send_d,
+                  recv_d, last, own_sem, sib_send, sib_recv, a_send, a_recv, b_send, b_recv, c_send, c_recv, d_send,
+                  d_recv):
+    tilt, slab = lax.axis_index("tilt"), lax.axis_index("slab")
+    core, z, x = tilt % 2, tilt // 2 % ZS, tilt // (2 * ZS)
+
+    def at_z(step):
+        return (x * (2 * ZS) + (z + step + ZS) % ZS * 2 + core, slab)
+
+    def at_x(step):
+        return ((x + step + XS) % XS * (2 * ZS) + z * 2 + core, slab)
+
+    twin = (tilt + 1 - 2 * core, slab)
+    barrier = pltpu.get_barrier_semaphore()
+    for device in (twin, at_z(1), at_z(-1), at_x(1), at_x(-1)):
+        pl.semaphore_signal(barrier, inc=1, device_id=device, device_id_type=pl.DeviceIdType.MESH)
+
+    own_copies = []
+    for q in (0, 1, 2, 3):
+        copy = pltpu.make_async_copy(
+            table_ref.at[pl.ds(pl.multiple_of((core * 4 + q) * PART_ROWS, PART_ROWS), PART_ROWS)],
+            own.at[pl.ds(q * PART_ROWS, PART_ROWS)], own_sem.at[q])
+        copy.start()
+        own_copies.append(copy)
+    pl.semaphore_wait(barrier, 5)
+
+    def ring(q, n, size, here, at, sign, plain, send, recv, send_sem, recv_sem):
+        half = n // 2
+
+        def slot_of(kind, j):
+            return j - 1 if kind == "major" else half + j - 1
+
+        def copy_of(kind, j):
+            slot = slot_of(kind, j)
+            return pltpu.make_async_remote_copy(
+                src_ref=send.at[q % 2, slot], dst_ref=recv.at[q % 2, slot],
+                send_sem=send_sem.at[q % 2, slot], recv_sem=recv_sem.at[q % 2, slot],
+                device_id=at(sign if kind == "major" else -sign), device_id_type=pl.DeviceIdType.MESH)
+
+        def owner_of(kind, j):
+            shift = sign * (half + 1 - j) if kind == "major" else -sign * (half - j)
+            return (here + shift + n) % n
+
+        def step(kind, j):
+            o = owner_of(kind, j)
+            slot = slot_of(kind, j)
+            if j > 1:
+                copy_of(kind, j - 1).wait_recv()
+
+            def tile(i, carry):
+                rows = pl.ds(pl.multiple_of(i * BOX, BOX), BOX)
+                total = plain(o, i)
+                if j > 1:
+                    total = total + recv[q % 2, slot - 1, rows, :].astype(jnp.float32)
+                send[q % 2, slot, rows, :] = total.astype(jnp.bfloat16)
+                return carry
+
+            lax.fori_loop(0, size // BOX, tile, 0)
+            copy_of(kind, j).start()
+
+        def final(store):
+            copy_of("major", half).wait_recv()
+            copy_of("minor", half - 1).wait_recv()
+
+            def tile(i, carry):
+                rows = pl.ds(pl.multiple_of(i * BOX, BOX), BOX)
+                store(i, plain(here, i) + recv[q % 2, half - 1, rows, :].astype(jnp.float32)
+                      + recv[q % 2, n - 2, rows, :].astype(jnp.float32))
+                return carry
+
+            lax.fori_loop(0, size // BOX, tile, 0)
+
+        def drain():
+            for kind, steps in (("major", half), ("minor", half - 1)):
+                for j in range(1, steps + 1):
+                    copy_of(kind, j).wait_send()
+
+        return step, final, drain, owner_of
+
+    A, B = XS * BOX, ZS * BOX
+    twin_copies = {}
+
+    def twin_copy(q, kind, j, o, size):
+        index = len(twin_copies)
+        rows = pl.multiple_of(q * PART_ROWS + o * size, size)
+        copy = pltpu.make_async_remote_copy(
+            src_ref=table_ref.at[pl.ds(pl.multiple_of((1 - core) * 4 * PART_ROWS + rows, size), size)],
+            dst_ref=sib.at[pl.ds(rows, size)], send_sem=sib_send.at[index], recv_sem=sib_recv.at[index],
+            device_id=twin, device_id_type=pl.DeviceIdType.MESH)
+        copy.start()
+        twin_copies[q, kind, j] = copy
+
+    def plain_first(q, size):
+        def plain(o, i):
+            rows = pl.ds(pl.multiple_of(q * PART_ROWS + o * size + i * BOX, BOX), BOX)
+            return own[rows, :].astype(jnp.float32) + sib[rows, :].astype(jnp.float32)
+        return plain
+
+    first, second = [], []
+    for q in range(4):
+        sign = 1 if q % 2 == 0 else -1
+        if q < 2:
+            first.append(ring(q, ZS, A, z, at_z, sign, plain_first(q, A), send_a, recv_a, a_send, a_recv))
+            second.append(ring(q, XS, BOX, x, at_x, sign,
+                               lambda o, i, q=q: mid_a[q % 2, pl.ds(pl.multiple_of(o * BOX, BOX), BOX), :],
+                               send_c, recv_c, c_send, c_recv))
+        else:
+            first.append(ring(q, XS, B, x, at_x, sign, plain_first(q, B), send_b, recv_b, b_send, b_recv))
+            second.append(ring(q, ZS, BOX, z, at_z, sign,
+                               lambda o, i, q=q: mid_b[q % 2, pl.ds(pl.multiple_of(o * BOX, BOX), BOX), :],
+                               send_d, recv_d, d_send, d_recv))
+
+    order = []
+    for kind in ("major", "minor"):
+        order += [(0, kind, 1), (1, kind, 1)]
+    order += [(2, "major", 1), (3, "major", 1), (2, "minor", 1), (3, "minor", 1)]
+    order += [(0, "major", 2), (1, "major", 2), (0, "minor", 2), (1, "minor", 2)]
+    order += [(2, "major", 2), (3, "major", 2)]
+    for j in (3,):
+        order += [(0, "major", j), (1, "major", j), (0, "minor", j), (1, "minor", j)]
+    order += [(0, "major", 4), (1, "major", 4)]
+    order += [(2, "own", 0), (3, "own", 0), (0, "own", 0), (1, "own", 0)]
+
+    for q, kind, j in order:
+        o = (z if q < 2 else x) if kind == "own" else first[q][3](kind, j)
+        twin_copy(q, kind, j, o, A if q < 2 else B)
+
+    waited = set()
+    for q, kind, j in order:
+        if q not in waited:
+            own_copies[q].wait()
+            waited.add(q)
+        twin_copies[q, kind, j].wait_recv()
+        if kind != "own":
+            first[q][0](kind, j)
+        else:
+            def store(i, value, q=q):
+                mid = mid_a if q < 2 else mid_b
+                mid[q % 2, pl.ds(pl.multiple_of(i * BOX, BOX), BOX), :] = value
+            first[q][1](store)
+            second[q][0]("major", 1)
+            second[q][0]("minor", 1)
+    for j in (2, 3, 4):
+        for q in (2, 3):
+            second[q][0]("major", j)
+            if j < 4:
+                second[q][0]("minor", j)
+        if j == 2:
+            for q in (0, 1):
+                second[q][0]("major", j)
+
+    def store_last(i, value):
+        last[...] = value
+
+    for q in (0, 1, 2, 3):
+        second[q][1](store_last)
+        out_ref[0, q] = last[pl.ds(0, 64, stride=2), :]
+        out_ref[1, q] = last[pl.ds(1, 64, stride=2), :]
+    for q in range(4):
+        first[q][2]()
+        second[q][2]()
+    for copy in twin_copies.values():
+        copy.wait_send()
+
+
+def reduce_table(table):
+    dma = pltpu.SemaphoreType.DMA
+    A, B = XS * BOX, ZS * BOX
+    return pl.pallas_call(
+        reduce_kernel,
+        out_shape=jax.ShapeDtypeStruct((2, HALFMAPS, 64, BOX), jnp.float32),
+        in_specs=[pl.BlockSpec(memory_space=pl.ANY)],
+        out_specs=pl.BlockSpec(memory_space=pltpu.VMEM),
+        scratch_shapes=[
+            pltpu.VMEM((SPOTS // 2, BOX), jnp.bfloat16),
+            pltpu.VMEM((SPOTS // 2, BOX), jnp.bfloat16),
+            pltpu.VMEM((2, ZS - 1, A, BOX), jnp.bfloat16),
+            pltpu.VMEM((2, ZS - 1, A, BOX), jnp.bfloat16),
+            pltpu.VMEM((2, XS - 1, B, BOX), jnp.bfloat16),
+            pltpu.VMEM((2, XS - 1, B, BOX), jnp.bfloat16),
+            pltpu.VMEM((2, A, BOX), jnp.float32),
+            pltpu.VMEM((2, B, BOX), jnp.float32),
+            pltpu.VMEM((2, XS - 1, BOX, BOX), jnp.bfloat16),
+            pltpu.VMEM((2, XS - 1, BOX, BOX), jnp.bfloat16),
+            pltpu.VMEM((2, ZS - 1, BOX, BOX), jnp.bfloat16),
+            pltpu.VMEM((2, ZS - 1, BOX, BOX), jnp.bfloat16),
+            pltpu.VMEM((BOX, BOX), jnp.float32),
+            dma((4,)), dma((24,)), dma((24,)),
+            dma((2, ZS - 1)), dma((2, ZS - 1)), dma((2, XS - 1)), dma((2, XS - 1)),
+            dma((2, XS - 1)), dma((2, XS - 1)), dma((2, ZS - 1)), dma((2, ZS - 1)),
+        ],
+        compiler_params=pltpu.CompilerParams(
+            collective_id=0, has_side_effects=True, vmem_limit_bytes=40 * 2**20),
+        name="reduce_table",
+    )(table)
+
+
 def tables():
     cos_table, sin_table = fourier_tables(BOX)
     stacked = jnp.concatenate([cos_table, sin_table], 0)
@@ -170,9 +372,11 @@
 
 def places_of(rows, labels, slab_index, slab_count):
     owner, offset = rows // 64, rows % 64
-    owner_tilt = owner // slab_count
-    block = (owner_tilt % 2) * (TILTS // 2) + owner_tilt // 2
-    place = 2 * ((block * HALFMAPS + labels[:, None]) * 64 + offset)
+    tilt = owner // slab_count
+    core, z, x = tilt % 2, tilt // 2 % ZS, tilt // (2 * ZS)
+    label = labels[:, None]
+    chip = jnp.where(label < 2, z * XS + x, x * ZS + z)
+    place = 2 * (((core * HALFMAPS + label) * (TILTS // 2) + chip) * 64 + offset)
     return jnp.where(owner % slab_count == slab_index, place, -1 - lax.broadcasted_iota(jnp.int32, rows.shape, 1))
 
 
@@ -191,10 +395,7 @@
     places = places_of(rows, labels_all, slab_index, slab_count)
     stacked, mixed = tables()
     table = insert(corners[:, 0], visible, tilt_images[0], places, stacked, mixed, transfer_factors(defocus_all))
-    table = table.reshape(2, 4, 8, HALFMAPS, 64, 2, BOX).transpose(1, 2, 0, 3, 4, 5, 6).reshape(TILTS, -1, BOX)
-    own = lax.psum_scatter(table, "tilt", scatter_dimension=0, tiled=True)
-    own = own.reshape(HALFMAPS, 64, 2, BOX)
-    return own.transpose(2, 0, 1, 3).astype(jnp.float32)
+    return reduce_table(table)
 
 
 def solution(mesh):

time: 295 us -> 168 us (0.57)
  waiting for transfers between devices: 158 us -> 9.39 us
  Pallas kernels: 92.9 us -> 133 us
  between operations: 13.5 us -> 0.16 us
  local copies, waits for them, and re-layouts: 14.5 us -> 9.3 us
    reduce_scatter x1 -> x0, waiting for transfers between devices: 148 us -> none  [body(): own = lax.psum_scatter(table, 'tilt', scatter_dimension=0, tiled=True)]
    pallas_call x0 -> x1, Pallas kernels: none -> 55.1 us  [reduce_table(): pl.pallas_call(reduce_kernel, out_shape=jax.ShapeDtypeStruct((2, HALFMAPS...]
    pallas_call x1, Pallas kernels: 92.9 us -> 78.3 us  [insert(): pl.pallas_call(insert_kernel, out_shape=jax.ShapeDtypeStruct((2 * CELLS,...]
    reshape x1 -> x0, local copies, waits for them, and re-layouts: 8.58 us -> none  [body(): table.reshape(2, 4, 8, HALFMAPS, 64, 2, BOX).transpose(1, 2, 0, 3, 4, 5, 6)]
    unnamed x8 -> x11, local copies, waits for them, and re-layouts: 4.1 us -> 8.18 us
  transfers between devices with their start and end apart: 2 -> 1, of which waited for: 2 -> 1; matrix products, arithmetic and copies ran while one was open for 0% -> 1% of each run, Pallas kernels for 0% -> 0%
where the time goes in v2:
time: 168 us; the launch traced here: 167 us
  Pallas kernels  133 us (79%)
  starting transfers between devices  11.9 us (7%)
  waiting for transfers between devices  9.39 us (6%)
  local copies, waits for them, and re-layouts  9.3 us (6%)
  other arithmetic  3.33 us (2%)
    pallas_call x1, Pallas kernels, insert(): pl.pallas_call(insert_kernel, out_shape=jax.ShapeDtypeStruct((2 * CELLS,...  78.3 us
    pallas_call x1, Pallas kernels, reduce_table(): pl.pallas_call(reduce_kernel, out_shape=jax.ShapeDtypeStruct((2, HALFMAPS...  55.1 us
    all_to_all x1, starting transfers between devices, body(): lax.all_to_all(packed, 'tilt', split_axis=0, concat_axis=0, tiled=True)  11.9 us
    all_to_all x1, waiting for transfers between devices, body(): lax.all_to_all(packed, 'tilt', split_axis=0, concat_axis=0, tiled=True)  9.39 us
    unnamed x11, local copies, waits for them, and re-layouts  8.18 us
  transfers between devices with their start and end apart: 1, of which 1 were waited for; matrix products, arithmetic and copies ran while one was open for 1% of the time, Pallas kernels for 0%

profile of v2, /device:TPU:8, one launch (start us, length us, event | category | flops | bytes accessed | tf_op | source)
XLA Modules:
  0.0 167.5 jit_solution(14626573497470282060)
XLA Ops:
  0.0 0.7 convert_element_type.68
  0.7 0.9 copy.18
  1.6 0.9 copy.19
  2.5 0.1 stack_broadcast_in_dim.3
  2.6 0.7 select_maximum_fusion
  3.4 0.8 copy.20
  4.1 11.9 %all-to-all-start = ((f32[64,4,128]{2,1,0:T(4,128)}), f32[64,4,128]{2,1,0:T(4,128)S(1)}, u32[]{:S(2)}, u32[]{:S(2)}) async-start(f32[64,4,128]{2,1,0:T(4,128)} %copy.20), calls=%async_computation | async-start | bytes 262144 | tf_op jit(solution)/shard_map/all_to_all | solution.py:391
  16.1 0.3 fusion.44
  16.4 0.6 negate_convert_fusion
  17.0 9.4 %all-to-all-done = f32[64,4,128]{2,1,0:T(4,128)S(1)} async-done(((f32[64,4,128]{2,1,0:T(4,128)}), f32[64,4,128]{2,1,0:T(4,128)S(1)}, u32[]{:S(2)}, u32[]{:S(2)}) %all-to-all-start) | async-done | bytes 131104 | tf_op jit(solution)/shard_map/all_to_all | solution.py:391
  26.4 0.1 fusion.42
  26.5 0.1 mul.177
  26.6 0.1 fusion.43
  26.8 0.1 convert_element_type.72
  26.9 0.5 multiply_sine_fusion
  27.5 0.3 fusion.20.places_ref
  27.8 0.0 copy-start.1
  27.8 0.9 copy-done.1
  28.7 0.0 copy-start.2
  28.7 0.7 copy-done.2
  29.3 0.0 copy-start.3
  29.4 0.7 copy-done.3
  30.0 78.3 %insert_slices.1.table_ref = bf16[32768,128]{1,0:T(8,128)(2,1)} custom-call(s32[2,128]{1,0:T(2,128)S(1)} %bitcast.15, s32[1,128]{1,0:T(1,128)S(1)} %copy-done.3, bf16[256,256]{1,0:T(8,128)(2,1)S(1)} %bitcast.14, s32[128,128]{1,0:T(8,128)S(1)} %fusion.20.places_ref, bf16[256,128]{1,0:T(8,128)(2,1)S(1)} %pad_maximum_fusion.1.stacked_ref, ...), custom_call_target="tpu_custom_call" | custom-call | tf_op jit(solution)/shard_map/insert_slices/pallas_call | solution.py:138
  108.3 0.0 copy-start
  108.3 3.4 %copy-done = bf16[32768,128]{1,0:T(8,128)(2,1)S(1)} copy-done((bf16[32768,128]{1,0:T(8,128)(2,1)S(1)}, bf16[32768,128]{1,0:T(8,128)(2,1)}, u32[]{:S(2)}) %copy-start) | copy-done | bytes 8388632
  111.7 55.1 %reduce_table.1 = f32[2,4,64,128]{3,2,1,0:T(8,128)S(1)} custom-call(bf16[32768,128]{1,0:T(8,128)(2,1)S(1)} %copy-done), custom_call_target="tpu_custom_call" | custom-call | tf_op jit(solution)/shard_map/reduce_table/pallas_call | solution.py:335
  166.7 0.7 copy.22
  (9 shorter events, 0.1 us)
Async XLA Ops:
  4.1 22.2 %all-to-all-start = ((f32[64,4,128]{2,1,0:T(4,128)}), f32[64,4,128]{2,1,0:T(4,128)S(1)}, u32[]{:S(2)}, u32[]{:S(2)}) async-start(f32[64,4,128]{2,1,0:T(4,128)} %copy.20), calls=%async_computation | async-start | bytes 262144 | tf_op jit(solution)/shard_map/all_to_all | solution.py:391
  27.8 0.9 copy-start.1
  28.7 0.7 copy-start.2
  29.3 0.7 copy-start.3
  108.3 3.4 %copy-start = (bf16[32768,128]{1,0:T(8,128)(2,1)S(1)}, bf16[32768,128]{1,0:T(8,128)(2,1)}, u32[]{:S(2)}) copy-start(bf16[32768,128]{1,0:T(8,128)(2,1)} %insert_slices.1.table_ref) | copy-start | bytes 25165828

commit v3 on v2

--- a/solution.py
+++ b/solution.py
@@ -12,8 +12,10 @@
 TILTS = 64
 PARTICLES = 128
 CELLS = TILTS * HALFMAPS * 64
-GROUP = 16
+GROUP = 8
+PAIRS = PARTICLES // 2
 WINDOW = 2 * GROUP
+SLOTS = 64
 
 
 def fourier_tables(width):
@@ -35,25 +37,52 @@
 
 
 def insert_kernel(corner_ref, seen_ref, image_ref, places_ref, stacked_ref, mixed_ref, first_ref, second_ref,
-                  cos_ref, sin_ref, out_ref, left, right, main_list, late_list, late_any, main_s, late_s, any_s,
-                  slices_a, slices_b, table, sems):
+                  cos_ref, sin_ref, out_ref, left, right, lists, spans, late_rows, spot_s, row_s, late_s, span_s,
+                  late_rows_s, patches, sides, slices_a, slices_b, kept_slices, table, sems):
     lane = lax.broadcasted_iota(jnp.int32, (BOX, BOX), 1)
-    dump = 2 * CELLS + 2 * (lane % GROUP)
-    places = places_ref[...]
-    kept = places >= 0
-    later = jnp.zeros((BOX, BOX), jnp.bool_)
+    entry = lax.broadcasted_iota(jnp.int32, (8, BOX), 0)
+    rank = jnp.zeros((8, BOX), jnp.int32)
+    spots = [2 * CELLS + 2 * ((8 * s + entry) % (2 * GROUP)) for s in range(SLOTS // 8)]
+    spare = jnp.concatenate(spots, axis=0)
+    sources = [jnp.zeros((8, BOX), jnp.int32) for _ in range(SLOTS // 8)]
+    first_row, last_row = jnp.full((8, BOX), BOX, jnp.int32), jnp.zeros((8, BOX), jnp.int32)
+    for j in range(BOX // 8):
+        place = places_ref[8 * j:8 * j + 8, :]
+        kept = place >= 0
+        for s in range(SLOTS // 8):
+            hit = kept & (rank == s)
+            spots[s] = jnp.where(hit, place, spots[s])
+            sources[s] = jnp.where(hit, 2 * (8 * j + entry), sources[s])
+        over = kept & (rank >= SLOTS // 8)
+        late_rows[8 * j:8 * j + 8, :] = jnp.where(over, place, 2 * CELLS)
+        first_row = jnp.minimum(first_row, jnp.where(over, 8 * j + entry, BOX))
+        last_row = jnp.maximum(last_row, jnp.where(over, 8 * j + entry + 1, 0))
+        rank = rank + jnp.where(kept, 1, 0)
+    spot = jnp.concatenate(spots, axis=0)
+    slot = lax.broadcasted_iota(jnp.int32, (SLOTS, BOX), 0)
+    late = jnp.zeros((SLOTS, BOX), jnp.bool_)
     for d in range(1, WINDOW):
-        other = pltpu.roll(places, BOX - d, axis=1)
-        later = later | ((other == places) & (lane < BOX - d))
-    late = later & kept
-    main_list[...] = jnp.where(kept & ~late, places, dump)
-    late_list[...] = jnp.where(late, places, dump)
-    late_any[...] = jnp.broadcast_to(
-        jnp.max(jnp.where(late, 1, 0), axis=1, keepdims=True), (BOX, BOX))
+        late = late | ((pltpu.roll(spot, SLOTS - d, axis=0) == spot) & (slot < SLOTS - d))
+    lists[0, :, :BOX] = jnp.where(late, spare, spot)
+    lists[0, :, BOX:] = spare
+    lists[1, :, :BOX] = jnp.concatenate(sources, axis=0)
+    lists[1, :, BOX:] = jnp.zeros((SLOTS, BOX), jnp.int32)
+    lists[2, :, :BOX] = jnp.where(late, spot, spare)
+    lists[2, :, BOX:] = spare
+    row = lax.broadcasted_iota(jnp.int32, (8, BOX), 0)
+    bounds = [
+        jnp.min(jnp.where(late, slot, SLOTS), axis=0, keepdims=True),
+        jnp.max(jnp.where(late, slot + 1, 0), axis=0, keepdims=True),
+        jnp.min(first_row, axis=0, keepdims=True),
+        jnp.max(last_row, axis=0, keepdims=True),
+    ]
+    spans[...] = jnp.where(row == 0, bounds[0], jnp.where(row == 1, bounds[1], jnp.where(row == 2, bounds[2], bounds[3])))
     copies = [
-        pltpu.make_async_copy(main_list, main_s, sems.at[0]),
-        pltpu.make_async_copy(late_list, late_s, sems.at[1]),
-        pltpu.make_async_copy(late_any, any_s, sems.at[2]),
+        pltpu.make_async_copy(lists.at[0], spot_s, sems.at[0]),
+        pltpu.make_async_copy(lists.at[1], row_s, sems.at[1]),
+        pltpu.make_async_copy(lists.at[2], late_s, sems.at[2]),
+        pltpu.make_async_copy(spans, span_s, sems.at[3]),
+        pltpu.make_async_copy(late_rows, late_rows_s, sems.at[4]),
     ]
     for copy in copies:
         copy.start()
@@ -80,49 +109,74 @@
         scale = lax.rsqrt(variance + 1e-05) * seen_ref[0, p].astype(jnp.float32)
         return (centered * scale).astype(jnp.bfloat16)
 
-    def slices_of(pair):
-        p = 2 * pair
-        patches = jnp.concatenate([window(p), window(p + 1)], axis=1)
-        section = jnp.dot(stacked_ref[...], patches, preferred_element_type=jnp.float32).astype(jnp.bfloat16)
-        for j, target in ((0, slices_a), (1, slices_b)):
-            side = jnp.concatenate(
-                [section[:BOX, j * BOX:(j + 1) * BOX], section[BOX:, j * BOX:(j + 1) * BOX]], axis=1)
-            spectrum = jnp.dot(side, mixed_ref[...], preferred_element_type=jnp.float32)
+    def cut_pair(pair, target):
+        p = 2 * jnp.minimum(pair, PAIRS - 1)
+        target[:, :BOX] = window(p)
+        target[:, BOX:] = window(p + 1)
+
+    def first_pair(source, target):
+        section = jnp.dot(stacked_ref[...], source[...], preferred_element_type=jnp.float32).astype(jnp.bfloat16)
+        for j in range(2):
+            target[j * BOX:(j + 1) * BOX, :BOX] = section[:BOX, j * BOX:(j + 1) * BOX]
+            target[j * BOX:(j + 1) * BOX, BOX:] = section[BOX:, j * BOX:(j + 1) * BOX]
+
+    def second_pair(pair, source, targets):
+        p = 2 * jnp.clip(pair, 0, PAIRS - 1)
+        spectrum = jnp.dot(source[...], mixed_ref[...], preferred_element_type=jnp.float32)
+        for j, target in enumerate(targets):
             pick = jnp.full((BOX, BOX), p + j, jnp.int32)
             first = jnp.take_along_axis(first_ref[...], pick, axis=1)
             second = jnp.take_along_axis(second_ref[...], pick, axis=1)
             transfer = first * cos_ref[pl.ds(p + j, 1), :] + second * sin_ref[pl.ds(p + j, 1), :]
-            target[pl.ds(0, BOX, stride=2), :] = transfer * spectrum[:, :BOX]
-            target[pl.ds(1, BOX, stride=2), :] = transfer * spectrum[:, BOX:]
+            real = transfer * spectrum[j * BOX:(j + 1) * BOX, :BOX]
+            imag = transfer * spectrum[j * BOX:(j + 1) * BOX, BOX:]
+            target[pl.ds(0, BOX, stride=2), :] = real
+            target[pl.ds(1, BOX, stride=2), :] = imag
+            kept_slices[p + j, pl.ds(0, BOX, stride=2), :] = real
+            kept_slices[p + j, pl.ds(1, BOX, stride=2), :] = imag
 
     def insert(p, source):
         waiting = None
-        for g in range(BOX // GROUP + 1):
-            if g < BOX // GROUP:
-                spots = [main_s[p, g * GROUP + i] for i in range(GROUP)]
-                sums = [table[pl.ds(spots[i], 2), :] + source[pl.ds(2 * (g * GROUP + i), 2), :]
+        for g in range(SLOTS // GROUP + 1):
+            if g < SLOTS // GROUP:
+                spots = [spot_s[g * GROUP + i, p] for i in range(GROUP)]
+                sums = [table[pl.ds(spots[i], 2), :] + source[pl.ds(row_s[g * GROUP + i, p], 2), :]
                         for i in range(GROUP)]
             if waiting is not None:
                 for spot, total in zip(*waiting):
                     table[pl.ds(spot, 2), :] = total
             waiting = (spots, sums)
 
-        @pl.when(any_s[p, 0] > 0)
+    def insert_late(p, carry):
+        @pl.when(span_s[1, p] + span_s[3, p] > 0)
         def _():
-            def one(i, carry):
-                spot = late_s[p, i]
-                table[pl.ds(spot, 2), :] += source[pl.ds(2 * i, 2), :]
+            def from_slot(i, carry):
+                table[pl.ds(late_s[i, p], 2), :] += kept_slices[p, pl.ds(row_s[i, p], 2), :]
                 return carry
 
-            lax.fori_loop(0, BOX, one, 0)
-
-    def step(pair, carry):
-        slices_of(pair)
-        insert(2 * pair, slices_a)
-        insert(2 * pair + 1, slices_b)
+            def from_row(i, carry):
+                table[pl.ds(late_rows_s[i, p], 2), :] += kept_slices[p, pl.ds(2 * i, 2), :]
+                return carry
+
+            lax.fori_loop(span_s[0, p], span_s[1, p], from_slot, 0)
+            lax.fori_loop(span_s[2, p], span_s[3, p], from_row, 0)
+
         return carry
 
-    lax.fori_loop(0, PARTICLES // 2, step, 0)
+    def step(i, carry):
+        for h in range(2):
+            tick = 2 * i + h
+            done = tick - 3
+            p = 2 * jnp.where(done < 0, PAIRS, done)
+            insert(p, slices_a[1 - h])
+            insert(p + 1, slices_b[1 - h])
+            second_pair(tick - 2, sides[h], (slices_a[h], slices_b[h]))
+            first_pair(patches[1 - h], sides[1 - h])
+            cut_pair(tick, patches[h])
+        return carry
+
+    lax.fori_loop(0, (PAIRS + 4) // 2, step, 0)
+    lax.fori_loop(0, PARTICLES, insert_late, 0)
 
     def finish(i, carry):
         rows = pl.ds(pl.multiple_of(i * 512, 512), 512)
@@ -143,18 +197,23 @@
         scratch_shapes=[
             pltpu.VMEM((256, BOX), jnp.float32),
             pltpu.VMEM((256, BOX), jnp.float32),
+            pltpu.VMEM((3, SLOTS, 2 * BOX), jnp.int32),
+            pltpu.VMEM((8, BOX), jnp.int32),
             pltpu.VMEM((BOX, BOX), jnp.int32),
-            pltpu.VMEM((BOX, BOX), jnp.int32),
-            pltpu.VMEM((BOX, BOX), jnp.int32),
+            pltpu.SMEM((SLOTS, 2 * BOX), jnp.int32),
+            pltpu.SMEM((SLOTS, 2 * BOX), jnp.int32),
+            pltpu.SMEM((SLOTS, 2 * BOX), jnp.int32),
+            pltpu.SMEM((8, BOX), jnp.int32),
             pltpu.SMEM((BOX, BOX), jnp.int32),
-            pltpu.SMEM((BOX, BOX), jnp.int32),
-            pltpu.SMEM((BOX, BOX), jnp.int32),
-            pltpu.VMEM((2 * BOX, BOX), jnp.float32),
-            pltpu.VMEM((2 * BOX, BOX), jnp.float32),
-            pltpu.VMEM((2 * CELLS + 2 * GROUP, BOX), jnp.float32),
-            pltpu.SemaphoreType.DMA((3,)),
+            [pltpu.VMEM((BOX, 2 * BOX), jnp.bfloat16)] * 2,
+            [pltpu.VMEM((2 * BOX, 2 * BOX), jnp.bfloat16)] * 2,
+            [pltpu.VMEM((2 * BOX, BOX), jnp.float32)] * 2,
+            [pltpu.VMEM((2 * BOX, BOX), jnp.float32)] * 2,
+            pltpu.VMEM((PARTICLES, 2 * BOX, BOX), jnp.float32),
+            pltpu.VMEM((2 * CELLS + 4 * GROUP, BOX), jnp.float32),
+            pltpu.SemaphoreType.DMA((5,)),
         ],
-        compiler_params=pltpu.CompilerParams(vmem_limit_bytes=48 * 2**20),
+        compiler_params=pltpu.CompilerParams(vmem_limit_bytes=56 * 2**20),
         name="insert_slices",
     )(corners, seen, image, places, stacked, mixed, *factors)
 
@@ -356,7 +415,7 @@
             dma((2, XS - 1)), dma((2, XS - 1)), dma((2, ZS - 1)), dma((2, ZS - 1)),
         ],
         compiler_params=pltpu.CompilerParams(
-            collective_id=0, has_side_effects=True, vmem_limit_bytes=40 * 2**20),
+            collective_id=0, has_side_effects=True, vmem_limit_bytes=60 * 2**20),
         name="reduce_table",
     )(table)
 
@@ -377,7 +436,7 @@
     label = labels[:, None]
     chip = jnp.where(label < 2, z * XS + x, x * ZS + z)
     place = 2 * (((core * HALFMAPS + label) * (TILTS // 2) + chip) * 64 + offset)
-    return jnp.where(owner % slab_count == slab_index, place, -1 - lax.broadcasted_iota(jnp.int32, rows.shape, 1))
+    return jnp.where(owner % slab_count == slab_index, place, -1).T
 
 
 def body(tilt_images, corners, visible, defocus, labels, row_owner, row_offset):

time: 168 us -> 116 us (0.69)
  Pallas kernels: 133 us -> 84.6 us
  local copies, waits for them, and re-layouts: 9.3 us -> 5.39 us
  other arithmetic: 3.33 us -> 5.25 us
    pallas_call x1, Pallas kernels: 78.3 us -> 46.3 us  [insert(): pl.pallas_call(insert_kernel, out_shape=jax.ShapeDtypeStruct((2 * CELLS,...]
    pallas_call x1, Pallas kernels: 55.1 us -> 38.3 us  [reduce_table(): pl.pallas_call(reduce_kernel, out_shape=jax.ShapeDtypeStruct((2, HALFMAPS...]
    unnamed x11 -> x3, local copies, waits for them, and re-layouts: 8.18 us -> 3.54 us
  transfers between devices with their start and end apart: 1 -> 1, of which waited for: 1 -> 1; matrix products, arithmetic and copies ran while one was open for 1% -> 2% of each run, Pallas kernels for 0% -> 0%
where the time goes in v3:
time: 116 us; the launch traced here: 115 us
  Pallas kernels  84.6 us (73%)
  starting transfers between devices  11.9 us (10%)
  waiting for transfers between devices  8.15 us (7%)
  local copies, waits for them, and re-layouts  5.39 us (5%)
  other arithmetic  5.25 us (5%)
    pallas_call x1, Pallas kernels, insert(): pl.pallas_call(insert_kernel, out_shape=jax.ShapeDtypeStruct((2 * CELLS,...  46.3 us
    pallas_call x1, Pallas kernels, reduce_table(): pl.pallas_call(reduce_kernel, out_shape=jax.ShapeDtypeStruct((2, HALFMAPS...  38.3 us
    all_to_all x1, starting transfers between devices, body(): lax.all_to_all(packed, 'tilt', split_axis=0, concat_axis=0, tiled=True)  11.9 us
    all_to_all x1, waiting for transfers between devices, body(): lax.all_to_all(packed, 'tilt', split_axis=0, concat_axis=0, tiled=True)  8.15 us
    unnamed x3, local copies, waits for them, and re-layouts  3.54 us
  transfers between devices with their start and end apart: 1, of which 1 were waited for; matrix products, arithmetic and copies ran while one was open for 2% of the time, Pallas kernels for 0%

profile of v3, /device:TPU:8, one launch (start us, length us, event | category | flops | bytes accessed | tf_op | source)
XLA Modules:
  0.0 115.4 jit_solution(3453472278811464479)
XLA Ops:
  0.0 0.7 convert_element_type.68
  0.7 0.9 copy.20
  1.6 0.9 copy.21
  2.5 0.1 stack_broadcast_in_dim.3
  2.6 0.7 select_maximum_fusion
  3.4 0.8 copy.22
  4.1 11.9 %all-to-all-start = ((f32[64,4,128]{2,1,0:T(4,128)}), f32[64,4,128]{2,1,0:T(4,128)S(1)}, u32[]{:S(2)}, u32[]{:S(2)}) async-start(f32[64,4,128]{2,1,0:T(4,128)} %copy.22), calls=%async_computation | async-start | bytes 262144 | tf_op jit(solution)/shard_map/all_to_all | solution.py:450
  16.1 0.3 fusion.45
  16.4 0.6 negate_convert_fusion
  16.9 0.6 pad_maximum_fusion.1.stacked_ref
  17.6 0.7 maximum_maximum_fusion.mixed_ref
  18.2 8.2 %all-to-all-done = f32[64,4,128]{2,1,0:T(4,128)S(1)} async-done(((f32[64,4,128]{2,1,0:T(4,128)}), f32[64,4,128]{2,1,0:T(4,128)S(1)}, u32[]{:S(2)}, u32[]{:S(2)}) %all-to-all-start) | async-done | bytes 131104 | tf_op jit(solution)/shard_map/all_to_all | solution.py:450
  26.4 0.1 fusion.43
  26.5 0.1 mul.177
  26.6 0.1 fusion.44
  26.8 0.1 convert_element_type.72
  26.9 0.3 fusion.21
  27.2 0.7 copy.23.places_ref
  27.9 1.2 %multiply_sine_fusion = (f32[128,128]{1,0:T(8,128)}, f32[128,128]{1,0:T(8,128)}, f32[128,128]{1,0:T(8,128)}, f32[128,128]{1,0:T(8,128)}) fusion(f32[128]{0:T(128)S(1)} %multiply_multiply_fusion, f32[128]{0:T(128)S(1)} %mul.177), kind=kLoop, calls=%fused_computation.34 | loop fusion | flops 196608 | bytes 263168 | tf_op jit(solution)/shard_map/sin | solution.py:32
  29.1 46.3 %insert_slices.1.table_ref = bf16[32768,128]{1,0:T(8,128)(2,1)} custom-call(s32[2,128]{1,0:T(2,128)} %bitcast.19, s32[1,128]{1,0:T(1,128)} %seen_ref.1, bf16[256,256]{1,0:T(8,128)(2,1)} %bitcast.17, s32[128,128]{1,0:T(8,128)} %copy.23.places_ref, bf16[256,128]{1,0:T(8,128)(2,1)} %pad_maximum_fusion.1.stacked_ref, ...), custom_call_target="tpu_custom_call" | custom-call | tf_op jit(solution)/shard_map/insert_slices/pallas_call | solution.py:192
  75.5 38.3 %reduce_table.1 = f32[2,4,64,128]{3,2,1,0:T(8,128)} custom-call(bf16[32768,128]{1,0:T(8,128)(2,1)} %insert_slices.1.table_ref), custom_call_target="tpu_custom_call" | custom-call | tf_op jit(solution)/shard_map/reduce_table/pallas_call | solution.py:394
  113.7 1.7 %copy.25 = f32[2,4,64,128]{3,2,1,0:T(8,128)} copy(f32[2,4,64,128]{3,2,1,0:T(8,128)} %reduce_table.1) | data formatting | bytes 524288
  (6 shorter events, 0.1 us)
Async XLA Ops:
  4.1 22.2 %all-to-all-start = ((f32[64,4,128]{2,1,0:T(4,128)}), f32[64,4,128]{2,1,0:T(4,128)S(1)}, u32[]{:S(2)}, u32[]{:S(2)}) async-start(f32[64,4,128]{2,1,0:T(4,128)} %copy.22), calls=%async_computation | async-start | bytes 262144 | tf_op jit(solution)/shard_map/all_to_all | solution.py:450

commit v4 on v3

--- a/solution.py
+++ b/solution.py
@@ -1,3 +1,5 @@
+import math
+
 import jax
 import jax.numpy as jnp
 import numpy as np
@@ -16,6 +18,7 @@
 PAIRS = PARTICLES // 2
 WINDOW = 2 * GROUP
 SLOTS = 64
+CUTS = 4
 
 
 def fourier_tables(width):
@@ -26,20 +29,122 @@
     return (jnp.cos(angles).astype(jnp.bfloat16), (-jnp.sin(angles)).astype(jnp.bfloat16))
 
 
-def transfer_factors(defocus_values):
-    frequency = (jnp.arange(BOX, dtype=jnp.int32) - BOX // 2).astype(jnp.float32) / BOX
-    angle = jnp.pi * defocus_values[:, None] * (frequency * frequency)[None, :]
+def transfer_factors(defocus, column):
+    frequency = (column - BOX // 2).astype(jnp.float32) / BOX
+    angle = jnp.pi * defocus * (frequency * frequency)
     cos_part, sin_part = jnp.cos(angle), jnp.sin(angle)
-    main = jnp.sqrt(1.0 - AMPLITUDE * AMPLITUDE)
+    main = math.sqrt(1.0 - AMPLITUDE * AMPLITUDE)
     first = -(main * sin_part + AMPLITUDE * cos_part) / BOX
     second = -(main * cos_part - AMPLITUDE * sin_part) / BOX
-    return first.T, second.T, cos_part, sin_part
-
-
-def insert_kernel(corner_ref, seen_ref, image_ref, places_ref, stacked_ref, mixed_ref, first_ref, second_ref,
-                  cos_ref, sin_ref, out_ref, left, right, lists, spans, late_rows, spot_s, row_s, late_s, span_s,
-                  late_rows_s, patches, sides, slices_a, slices_b, kept_slices, table, sems):
+    return first, second, cos_part, sin_part
+
+
+def swap_kernel(corner_ref, seen_ref, image_ref, owner_ref, offset_ref, misc_ref, patches_ref, places_ref, first_ref,
+                second_ref, cos_ref, sin_ref, left, right, outbox, inbox, send_sem, recv_sem):
+    tilt, slab = lax.axis_index("tilt"), lax.axis_index("slab")
+    barrier = pltpu.get_barrier_semaphore()
+
+    def peer(d):
+        return (tilt + d) % TILTS
+
+    def greet(d, carry):
+        pl.semaphore_signal(barrier, inc=1, device_id=(peer(d), slab), device_id_type=pl.DeviceIdType.MESH)
+        return carry
+
+    lax.fori_loop(1, TILTS, greet, 0)
+    for j in range(2):
+        outbox[:, j, :] = (owner_ref[j] * 64 + offset_ref[j]).astype(jnp.float32)
+        outbox[:, 2 + j, :] = jnp.broadcast_to(misc_ref[j:j + 1, :], (TILTS, BOX))
+    pl.semaphore_wait(barrier, TILTS - 1)
+
+    def message(to, origin):
+        return pltpu.make_async_remote_copy(
+            src_ref=outbox.at[to], dst_ref=inbox.at[origin], send_sem=send_sem.at[to], recv_sem=recv_sem.at[origin],
+            device_id=(to, slab), device_id_type=pl.DeviceIdType.MESH)
+
+    def send(d, carry):
+        message(peer(d), tilt).start()
+        return carry
+
+    lax.fori_loop(1, TILTS, send, 0)
+    inbox[tilt] = outbox[tilt]
+    left[...] = image_ref[:, :BOX].astype(jnp.float32)
+    right[...] = image_ref[:, BOX:].astype(jnp.float32)
     lane = lax.broadcasted_iota(jnp.int32, (BOX, BOX), 1)
+
+    def window(p):
+        row, col = corner_ref[0, p], corner_ref[1, p]
+        a = left[pl.ds(row, BOX), :]
+        b = right[pl.ds(row, BOX), :]
+        cut = pltpu.roll(jnp.where(lane >= col, a, b), (BOX - col) % BOX, axis=1)
+        average = jnp.sum(jnp.sum(cut, axis=0, keepdims=True), axis=1, keepdims=True) * (1.0 / (BOX * BOX))
+        centered = cut - average
+        variance = jnp.sum(
+            jnp.sum(centered * centered, axis=0, keepdims=True), axis=1, keepdims=True) * (1.0 / (BOX * BOX))
+        scale = lax.rsqrt(variance + 1e-05) * seen_ref[0, p].astype(jnp.float32)
+        return (centered * scale).astype(jnp.bfloat16)
+
+    def cut_pairs(i, carry):
+        windows = [window(CUTS * i + j) for j in range(CUTS)]
+        for j, patch in enumerate(windows):
+            patches_ref[CUTS // 2 * i + j // 2, :, j % 2 * BOX:(j % 2 + 1) * BOX] = patch
+        return carry
+
+    lax.fori_loop(0, PARTICLES // CUTS, cut_pairs, 0)
+
+    def receive(d, carry):
+        message(tilt, peer(d)).wait_recv()
+        return carry
+
+    lax.fori_loop(1, TILTS, receive, 0)
+
+    rows = jnp.concatenate([inbox[:, 0, :], inbox[:, 1, :]], axis=0).astype(jnp.int32)
+    misc = jnp.concatenate([inbox[:, 2, :]] * 2, axis=0)
+    line = lax.broadcasted_iota(jnp.int32, (BOX, BOX), 0)
+    mine = jnp.where(lane == jnp.where(line < TILTS, tilt, TILTS + tilt), misc, 0.0)
+    defocus = jnp.sum(mine, axis=1, keepdims=True)
+    labels = jnp.concatenate([inbox[:, 3, :]] * 2, axis=0)
+    label = jnp.sum(jnp.where(lane == jnp.where(line < TILTS, 0, TILTS), labels, 0.0), axis=1, keepdims=True)
+    places_ref[...] = places_of(rows, label.astype(jnp.int32), slab, lax.axis_size("slab")).T
+    first, second, cos_part, sin_part = transfer_factors(defocus, lane)
+    first_ref[...] = first.T
+    second_ref[...] = second.T
+    cos_ref[...] = cos_part
+    sin_ref[...] = sin_part
+
+    def sent(d, carry):
+        message(peer(d), tilt).wait_send()
+        return carry
+
+    lax.fori_loop(1, TILTS, sent, 0)
+
+
+def swap(corners, seen, image, owners, offsets, misc):
+    whole = pl.BlockSpec(memory_space=pltpu.VMEM)
+    scalars = pl.BlockSpec(memory_space=pltpu.SMEM)
+    square = jax.ShapeDtypeStruct((BOX, BOX), jnp.float32)
+    return pl.pallas_call(
+        swap_kernel,
+        out_shape=[jax.ShapeDtypeStruct((PAIRS, BOX, 2 * BOX), jnp.bfloat16),
+                   jax.ShapeDtypeStruct((BOX, BOX), jnp.int32)] + [square] * 4,
+        in_specs=[scalars, scalars] + [whole] * 4,
+        out_specs=[whole] * 6,
+        scratch_shapes=[
+            pltpu.VMEM((256, BOX), jnp.float32),
+            pltpu.VMEM((256, BOX), jnp.float32),
+            pltpu.VMEM((TILTS, 4, BOX), jnp.float32),
+            pltpu.VMEM((TILTS, 4, BOX), jnp.float32),
+            pltpu.SemaphoreType.DMA((TILTS,)),
+            pltpu.SemaphoreType.DMA((TILTS,)),
+        ],
+        compiler_params=pltpu.CompilerParams(
+            collective_id=1, has_side_effects=True, vmem_limit_bytes=24 * 2**20),
+        name="swap_rows",
+    )(corners, seen, image, owners, offsets, misc)
+
+
+def insert_kernel(patches_ref, places_ref, stacked_ref, mixed_ref, first_ref, second_ref, cos_ref, sin_ref, out_ref,
+                  lists, spans, late_rows, spot_s, row_s, late_s, span_s, late_rows_s, sides, slices_a, slices_b, kept_slices, table, sems):
     entry = lax.broadcasted_iota(jnp.int32, (8, BOX), 0)
     rank = jnp.zeros((8, BOX), jnp.int32)
     spots = [2 * CELLS + 2 * ((8 * s + entry) % (2 * GROUP)) for s in range(SLOTS // 8)]
@@ -86,8 +191,6 @@
     ]
     for copy in copies:
         copy.start()
-    left[...] = image_ref[:, :BOX].astype(jnp.float32)
-    right[...] = image_ref[:, BOX:].astype(jnp.float32)
 
     def clear(i, carry):
         table[pl.ds(pl.multiple_of(i * 512, 512), 512), :] = jnp.zeros((512, BOX), jnp.float32)
@@ -97,43 +200,28 @@
     for copy in copies:
         copy.wait()
 
-    def window(p):
-        row, col = corner_ref[0, p], corner_ref[1, p]
-        a = left[pl.ds(row, BOX), :]
-        b = right[pl.ds(row, BOX), :]
-        cut = pltpu.roll(jnp.where(lane >= col, a, b), (BOX - col) % BOX, axis=1)
-        average = jnp.sum(jnp.sum(cut, axis=0, keepdims=True), axis=1, keepdims=True) * (1.0 / (BOX * BOX))
-        centered = cut - average
-        variance = jnp.sum(
-            jnp.sum(centered * centered, axis=0, keepdims=True), axis=1, keepdims=True) * (1.0 / (BOX * BOX))
-        scale = lax.rsqrt(variance + 1e-05) * seen_ref[0, p].astype(jnp.float32)
-        return (centered * scale).astype(jnp.bfloat16)
-
-    def cut_pair(pair, target):
-        p = 2 * jnp.minimum(pair, PAIRS - 1)
-        target[:, :BOX] = window(p)
-        target[:, BOX:] = window(p + 1)
-
-    def first_pair(source, target):
-        section = jnp.dot(stacked_ref[...], source[...], preferred_element_type=jnp.float32).astype(jnp.bfloat16)
+    def line(pair, j):
+        return j * PAIRS + pair
+
+    def first_pair(patch, target):
+        section = jnp.dot(stacked_ref[...], patch, preferred_element_type=jnp.float32).astype(jnp.bfloat16)
         for j in range(2):
             target[j * BOX:(j + 1) * BOX, :BOX] = section[:BOX, j * BOX:(j + 1) * BOX]
             target[j * BOX:(j + 1) * BOX, BOX:] = section[BOX:, j * BOX:(j + 1) * BOX]
 
-    def second_pair(pair, source, targets):
-        p = 2 * jnp.clip(pair, 0, PAIRS - 1)
+    def second_pair(pair, rows, source, targets):
         spectrum = jnp.dot(source[...], mixed_ref[...], preferred_element_type=jnp.float32)
         for j, target in enumerate(targets):
-            pick = jnp.full((BOX, BOX), p + j, jnp.int32)
+            pick = jnp.full((BOX, BOX), line(pair, j), jnp.int32)
             first = jnp.take_along_axis(first_ref[...], pick, axis=1)
             second = jnp.take_along_axis(second_ref[...], pick, axis=1)
-            transfer = first * cos_ref[pl.ds(p + j, 1), :] + second * sin_ref[pl.ds(p + j, 1), :]
+            transfer = first * rows[j][0] + second * rows[j][1]
             real = transfer * spectrum[j * BOX:(j + 1) * BOX, :BOX]
             imag = transfer * spectrum[j * BOX:(j + 1) * BOX, BOX:]
             target[pl.ds(0, BOX, stride=2), :] = real
             target[pl.ds(1, BOX, stride=2), :] = imag
-            kept_slices[p + j, pl.ds(0, BOX, stride=2), :] = real
-            kept_slices[p + j, pl.ds(1, BOX, stride=2), :] = imag
+            kept_slices[line(pair, j), pl.ds(0, BOX, stride=2), :] = real
+            kept_slices[line(pair, j), pl.ds(1, BOX, stride=2), :] = imag
 
     def insert(p, source):
         waiting = None
@@ -166,16 +254,17 @@
     def step(i, carry):
         for h in range(2):
             tick = 2 * i + h
-            done = tick - 3
-            p = 2 * jnp.where(done < 0, PAIRS, done)
-            insert(p, slices_a[1 - h])
-            insert(p + 1, slices_b[1 - h])
-            second_pair(tick - 2, sides[h], (slices_a[h], slices_b[h]))
-            first_pair(patches[1 - h], sides[1 - h])
-            cut_pair(tick, patches[h])
-        return carry
-
-    lax.fori_loop(0, (PAIRS + 4) // 2, step, 0)
+            patch = patches_ref[jnp.minimum(tick, PAIRS - 1)]
+            pair = jnp.clip(tick - 1, 0, PAIRS - 1)
+            rows = [(cos_ref[pl.ds(line(pair, j), 1), :], sin_ref[pl.ds(line(pair, j), 1), :]) for j in range(2)]
+            idle = (tick < 2) | (tick >= PAIRS + 2)
+            insert(jnp.where(idle, PARTICLES, tick - 2), slices_a[h])
+            insert(jnp.where(idle, PARTICLES, line(tick - 2, 1)), slices_b[h])
+            first_pair(patch, sides[h])
+            second_pair(pair, rows, sides[1 - h], (slices_a[1 - h], slices_b[1 - h]))
+        return carry
+
+    lax.fori_loop(0, (PAIRS + 2) // 2, step, 0)
     lax.fori_loop(0, PARTICLES, insert_late, 0)
 
     def finish(i, carry):
@@ -186,17 +275,14 @@
     lax.fori_loop(0, 2 * CELLS // 512, finish, 0)
 
 
-def insert(corners, seen, image, places, stacked, mixed, factors):
+def insert(patches, places, stacked, mixed, factors):
     whole = pl.BlockSpec(memory_space=pltpu.VMEM)
-    scalars = pl.BlockSpec(memory_space=pltpu.SMEM)
     return pl.pallas_call(
         insert_kernel,
         out_shape=jax.ShapeDtypeStruct((2 * CELLS, BOX), jnp.bfloat16),
-        in_specs=[scalars, scalars] + [whole] * 8,
+        in_specs=[whole] * 8,
         out_specs=whole,
         scratch_shapes=[
-            pltpu.VMEM((256, BOX), jnp.float32),
-            pltpu.VMEM((256, BOX), jnp.float32),
             pltpu.VMEM((3, SLOTS, 2 * BOX), jnp.int32),
             pltpu.VMEM((8, BOX), jnp.int32),
             pltpu.VMEM((BOX, BOX), jnp.int32),
@@ -205,7 +291,6 @@
             pltpu.SMEM((SLOTS, 2 * BOX), jnp.int32),
             pltpu.SMEM((8, BOX), jnp.int32),
             pltpu.SMEM((BOX, BOX), jnp.int32),
-            [pltpu.VMEM((BOX, 2 * BOX), jnp.bfloat16)] * 2,
             [pltpu.VMEM((2 * BOX, 2 * BOX), jnp.bfloat16)] * 2,
             [pltpu.VMEM((2 * BOX, BOX), jnp.float32)] * 2,
             [pltpu.VMEM((2 * BOX, BOX), jnp.float32)] * 2,
@@ -213,9 +298,9 @@
             pltpu.VMEM((2 * CELLS + 4 * GROUP, BOX), jnp.float32),
             pltpu.SemaphoreType.DMA((5,)),
         ],
-        compiler_params=pltpu.CompilerParams(vmem_limit_bytes=56 * 2**20),
+        compiler_params=pltpu.CompilerParams(vmem_limit_bytes=46 * 2**20),
         name="insert_slices",
-    )(corners, seen, image, places, stacked, mixed, *factors)
+    )(patches, places, stacked, mixed, *factors)
 
 
 ZS, XS = 8, 4
@@ -433,28 +518,18 @@
     owner, offset = rows // 64, rows % 64
     tilt = owner // slab_count
     core, z, x = tilt % 2, tilt // 2 % ZS, tilt // (2 * ZS)
-    label = labels[:, None]
+    label = labels
     chip = jnp.where(label < 2, z * XS + x, x * ZS + z)
     place = 2 * (((core * HALFMAPS + label) * (TILTS // 2) + chip) * 64 + offset)
-    return jnp.where(owner % slab_count == slab_index, place, -1).T
+    return jnp.where(owner % slab_count == slab_index, place, -1)
 
 
 def body(tilt_images, corners, visible, defocus, labels, row_owner, row_offset):
-    slab_count = lax.axis_size("slab")
-    slab_index = lax.axis_index("slab")
-    rows = (row_owner[..., 0] * 64 + row_offset).astype(jnp.float32)
-    packed = jnp.concatenate([
-        rows.transpose(1, 0, 2),
-        jnp.pad(jnp.stack([defocus.T, jnp.broadcast_to(labels.astype(jnp.float32), (TILTS, 2))], 1),
-                ((0, 0), (0, 0), (0, BOX - 2)))], 1)
-    packed = lax.all_to_all(packed, "tilt", split_axis=0, concat_axis=0, tiled=True)
-    rows = packed[:, :2].reshape(PARTICLES, BOX).astype(jnp.int32)
-    defocus_all = packed[:, 2, :2].reshape(PARTICLES)
-    labels_all = packed[:, 3, :2].reshape(PARTICLES).astype(jnp.int32)
-    places = places_of(rows, labels_all, slab_index, slab_count)
+    misc = jnp.stack([defocus.reshape(BOX), jnp.repeat(labels.astype(jnp.float32), TILTS)])
+    patches, places, *factors = swap(
+        corners[:, 0], visible, tilt_images[0], row_owner[..., 0], row_offset, misc)
     stacked, mixed = tables()
-    table = insert(corners[:, 0], visible, tilt_images[0], places, stacked, mixed, transfer_factors(defocus_all))
-    return reduce_table(table)
+    return reduce_table(insert(patches, places, stacked, mixed, factors))
 
 
 def solution(mesh):

time: 116 us -> 111 us (0.957)
  Pallas kernels: 84.6 us -> 102 us
  starting transfers between devices: 11.9 us -> 0 us
  waiting for transfers between devices: 8.15 us -> 0 us
  other arithmetic: 5.25 us -> 1.52 us
    pallas_call x0 -> x1, Pallas kernels: none -> 26.3 us  [swap(): pl.pallas_call(swap_kernel, out_shape=[jax.ShapeDtypeStruct((PAIRS, BOX,...]
    all_to_all x1 -> x0, starting transfers between devices: 11.9 us -> none  [body(): lax.all_to_all(packed, 'tilt', split_axis=0, concat_axis=0, tiled=True)]
    pallas_call x1, Pallas kernels: 46.3 us -> 37.3 us  [insert(): pl.pallas_call(insert_kernel, out_shape=jax.ShapeDtypeStruct((2 * CELLS,...]
    all_to_all x1 -> x0, waiting for transfers between devices: 8.15 us -> none  [body(): lax.all_to_all(packed, 'tilt', split_axis=0, concat_axis=0, tiled=True)]
    unnamed x3 -> x11, local copies, waits for them, and re-layouts: 3.54 us -> 5.58 us
    sin x1 -> x0, other arithmetic: 1.21 us -> none  [transfer_factors(): cos_part, sin_part = (jnp.cos(angle), jnp.sin(angle))]
  transfers between devices with their start and end apart: 1 -> 0, of which waited for: 1 -> 0; matrix products, arithmetic and copies ran while one was open for 2% -> 0% of each run, Pallas kernels for 0% -> 0%
where the time goes in v4:
time: 111 us; the launch traced here: 110 us
  Pallas kernels  102 us (92%)
  local copies, waits for them, and re-layouts  6.5 us (6%)
  other arithmetic  1.52 us (1%)
    pallas_call x1, Pallas kernels, reduce_table(): pl.pallas_call(reduce_kernel, out_shape=jax.ShapeDtypeStruct((2, HALFMAPS...  38 us
    pallas_call x1, Pallas kernels, insert(): pl.pallas_call(insert_kernel, out_shape=jax.ShapeDtypeStruct((2 * CELLS,...  37.3 us
    pallas_call x1, Pallas kernels, swap(): pl.pallas_call(swap_kernel, out_shape=[jax.ShapeDtypeStruct((PAIRS, BOX,...  26.3 us
    unnamed x11, local copies, waits for them, and re-layouts  5.58 us

profile of v4, /device:TPU:8, one launch (start us, length us, event | category | flops | bytes accessed | tf_op | source)
XLA Modules:
  0.0 109.7 jit_solution(5596451059461010920)
XLA Ops:
  0.0 0.8 stack_reshape.6
  0.8 0.7 convert_element_type.34
  1.4 0.1 broadcast_in_dim.2
  1.5 0.1 stack_reshape.7
  1.6 0.3 fusion.12
  1.9 0.6 negate_convert_fusion
  2.5 0.0 copy-start
  2.5 0.9 copy-done
  3.4 0.0 copy-start.1
  3.4 0.8 copy-done.1
  4.2 0.0 copy-start.2
  4.2 0.8 copy-done.2
  5.0 0.0 copy-start.3
  5.1 0.7 copy-done.3
  5.7 0.0 copy-start.4
  5.7 0.7 copy-done.4
  6.4 26.3 %swap_rows.1 = (bf16[64,128,256]{2,1,0:T(8,128)(2,1)S(1)}, s32[128,128]{1,0:T(8,128)S(1)}, f32[128,128]{1,0:T(8,128)S(1)}, f32[128,128]{1,0:T(8,128)S(1)}, f32[1...) custom-call(s32[2,128]{1,0:T(2,128)S(1)} %bitcast.5, s32[1,128]{1,0:T(1,128)S(1)} %copy-done.4, bf16[256,256]{1,0:T(8,128)(2,1)S(1)} %bitcast.3, ...), custom_call_target="tpu_custom_call" | custom-call | tf_op jit(solution)/shard_map/swap_rows/pallas_call | solution.py:126
  32.7 37.3 %insert_slices.1.table_ref = bf16[32768,128]{1,0:T(8,128)(2,1)} custom-call(bf16[64,128,256]{2,1,0:T(8,128)(2,1)S(1)} %get-tuple-element.11.patches_ref, s32[128,128]{1,0:T(8,128)S(1)} %get-tuple-element.12.places_ref, bf16[256,128]{1,0:T(8,128)(2,1)S(1)} %pad_maximum_fusion.stacked_ref, bf16[256,256]{1,0:T(8,128)(2,1)S(1)} %maximum_maximum_fusion.mixed_ref, ...), custom_call_target="tpu_custom_call" | custom-call | tf_op jit(solution)/shard_map/insert_slices/pallas_call | solution.py:280
  70.0 38.0 %reduce_table.1 = f32[2,4,64,128]{3,2,1,0:T(8,128)} custom-call(bf16[32768,128]{1,0:T(8,128)(2,1)} %insert_slices.1.table_ref), custom_call_target="tpu_custom_call" | custom-call | tf_op jit(solution)/shard_map/reduce_table/pallas_call | solution.py:479
  108.0 1.7 %copy.9 = f32[2,4,64,128]{3,2,1,0:T(8,128)} copy(f32[2,4,64,128]{3,2,1,0:T(8,128)} %reduce_table.1) | data formatting | bytes 524288
  (4 shorter events, 0.0 us)
Async XLA Ops:
  2.5 0.9 copy-start
  3.4 0.8 copy-start.1
  4.2 0.8 copy-start.2
  5.0 0.7 copy-start.3
  5.7 0.7 copy-start.4

commit v5 on v4

--- a/solution.py
+++ b/solution.py
@@ -18,7 +18,8 @@
 PAIRS = PARTICLES // 2
 WINDOW = 2 * GROUP
 SLOTS = 64
-CUTS = 4
+CUTS = 8
+CHUNK = 4096
 
 
 def fourier_tables(width):
@@ -39,8 +40,15 @@
     return first, second, cos_part, sin_part
 
 
-def swap_kernel(corner_ref, seen_ref, image_ref, owner_ref, offset_ref, misc_ref, patches_ref, places_ref, first_ref,
-                second_ref, cos_ref, sin_ref, left, right, outbox, inbox, send_sem, recv_sem):
+def swap_kernel(corner_hbm, seen_hbm, image_hbm, owner_hbm, offset_hbm, defocus_hbm, label_hbm, patches_hbm, places_ref,
+                first_ref, second_ref, cos_ref, sin_ref, corner_ref, seen_ref, image_ref, owner_ref, offset_ref,
+                defocus_ref, label_ref, left, right, outbox, inbox, patches_ref, send_sem, recv_sem, load_sem, store_sem):
+    loads = [
+        pltpu.make_async_copy(source, target, load_sem.at[i]) for i, (source, target) in enumerate((
+            (owner_hbm, owner_ref), (offset_hbm, offset_ref), (defocus_hbm, defocus_ref), (label_hbm, label_ref),
+            (image_hbm, image_ref), (corner_hbm, corner_ref), (seen_hbm, seen_ref)))]
+    for load in loads:
+        load.start()
     tilt, slab = lax.axis_index("tilt"), lax.axis_index("slab")
     barrier = pltpu.get_barrier_semaphore()
 
@@ -52,9 +60,13 @@
         return carry
 
     lax.fori_loop(1, TILTS, greet, 0)
+    for load in loads[:4]:
+        load.wait()
+    column = lax.broadcasted_iota(jnp.int32, (TILTS, BOX), 1)
     for j in range(2):
         outbox[:, j, :] = (owner_ref[j] * 64 + offset_ref[j]).astype(jnp.float32)
-        outbox[:, 2 + j, :] = jnp.broadcast_to(misc_ref[j:j + 1, :], (TILTS, BOX))
+        outbox[:, 2, j * TILTS:(j + 1) * TILTS] = jnp.broadcast_to(defocus_ref[j:j + 1, :], (TILTS, TILTS))
+    outbox[:, 3, :] = jnp.where(column < TILTS, label_ref[0, 0], label_ref[0, 1]).astype(jnp.float32)
     pl.semaphore_wait(barrier, TILTS - 1)
 
     def message(to, origin):
@@ -68,6 +80,8 @@
 
     lax.fori_loop(1, TILTS, send, 0)
     inbox[tilt] = outbox[tilt]
+    for load in loads[4:]:
+        load.wait()
     left[...] = image_ref[:, :BOX].astype(jnp.float32)
     right[...] = image_ref[:, BOX:].astype(jnp.float32)
     lane = lax.broadcasted_iota(jnp.int32, (BOX, BOX), 1)
@@ -84,10 +98,15 @@
         scale = lax.rsqrt(variance + 1e-05) * seen_ref[0, p].astype(jnp.float32)
         return (centered * scale).astype(jnp.bfloat16)
 
+    def leave(i):
+        pairs = pl.ds(CUTS // 2 * i, CUTS // 2)
+        return pltpu.make_async_copy(patches_ref.at[pairs], patches_hbm.at[pairs], store_sem.at[i])
+
     def cut_pairs(i, carry):
         windows = [window(CUTS * i + j) for j in range(CUTS)]
         for j, patch in enumerate(windows):
             patches_ref[CUTS // 2 * i + j // 2, :, j % 2 * BOX:(j % 2 + 1) * BOX] = patch
+        leave(i).start()
         return carry
 
     lax.fori_loop(0, PARTICLES // CUTS, cut_pairs, 0)
@@ -118,33 +137,50 @@
 
     lax.fori_loop(1, TILTS, sent, 0)
 
-
-def swap(corners, seen, image, owners, offsets, misc):
+    def left_all(i, carry):
+        leave(i).wait()
+        return carry
+
+    lax.fori_loop(0, PARTICLES // CUTS, left_all, 0)
+
+
+def swap(*operands):
     whole = pl.BlockSpec(memory_space=pltpu.VMEM)
-    scalars = pl.BlockSpec(memory_space=pltpu.SMEM)
     square = jax.ShapeDtypeStruct((BOX, BOX), jnp.float32)
     return pl.pallas_call(
         swap_kernel,
         out_shape=[jax.ShapeDtypeStruct((PAIRS, BOX, 2 * BOX), jnp.bfloat16),
                    jax.ShapeDtypeStruct((BOX, BOX), jnp.int32)] + [square] * 4,
-        in_specs=[scalars, scalars] + [whole] * 4,
-        out_specs=[whole] * 6,
+        in_specs=[pl.BlockSpec(memory_space=pltpu.HBM)] * 7,
+        out_specs=[pl.BlockSpec(memory_space=pltpu.HBM)] + [whole] * 5,
         scratch_shapes=[
+            pltpu.SMEM((2, BOX), jnp.int32),
+            pltpu.SMEM((1, BOX), jnp.int32),
+            pltpu.VMEM((256, 256), jnp.bfloat16),
+            pltpu.VMEM((2, TILTS, BOX), jnp.int32),
+            pltpu.VMEM((2, TILTS, BOX), jnp.int32),
+            pltpu.VMEM((2, TILTS), jnp.float32),
+            pltpu.SMEM((1, 2), jnp.int32),
             pltpu.VMEM((256, BOX), jnp.float32),
             pltpu.VMEM((256, BOX), jnp.float32),
             pltpu.VMEM((TILTS, 4, BOX), jnp.float32),
             pltpu.VMEM((TILTS, 4, BOX), jnp.float32),
+            pltpu.VMEM((PAIRS, BOX, 2 * BOX), jnp.bfloat16),
             pltpu.SemaphoreType.DMA((TILTS,)),
             pltpu.SemaphoreType.DMA((TILTS,)),
+            pltpu.SemaphoreType.DMA((7,)),
+            pltpu.SemaphoreType.DMA((PARTICLES // CUTS,)),
         ],
         compiler_params=pltpu.CompilerParams(
-            collective_id=1, has_side_effects=True, vmem_limit_bytes=24 * 2**20),
+            collective_id=1, has_side_effects=True, vmem_limit_bytes=62 * 2**20),
         name="swap_rows",
-    )(corners, seen, image, owners, offsets, misc)
-
-
-def insert_kernel(patches_ref, places_ref, stacked_ref, mixed_ref, first_ref, second_ref, cos_ref, sin_ref, out_ref,
-                  lists, spans, late_rows, spot_s, row_s, late_s, span_s, late_rows_s, sides, slices_a, slices_b, kept_slices, table, sems):
+    )(*operands)
+
+
+def insert_kernel(patches_hbm, places_ref, stacked_ref, mixed_ref, first_ref, second_ref, cos_ref, sin_ref, out_ref,
+                  lists, spans, late_rows, spot_s, row_s, late_s, span_s, late_rows_s, sides, slices_a, slices_b, staged, kept_slices, table, patches_ref, sems):
+    fetch = pltpu.make_async_copy(patches_hbm, patches_ref, sems.at[5])
+    fetch.start()
     entry = lax.broadcasted_iota(jnp.int32, (8, BOX), 0)
     rank = jnp.zeros((8, BOX), jnp.int32)
     spots = [2 * CELLS + 2 * ((8 * s + entry) % (2 * GROUP)) for s in range(SLOTS // 8)]
@@ -182,6 +218,10 @@
         jnp.max(last_row, axis=0, keepdims=True),
     ]
     spans[...] = jnp.where(row == 0, bounds[0], jnp.where(row == 1, bounds[1], jnp.where(row == 2, bounds[2], bounds[3])))
+    amount = bounds[1] + bounds[3]
+    for shift in (1, 2, 4, 8):
+        amount = amount + pltpu.roll(amount, BOX - shift, axis=1)
+    spans[4:5, :] = amount
     copies = [
         pltpu.make_async_copy(lists.at[0], spot_s, sems.at[0]),
         pltpu.make_async_copy(lists.at[1], row_s, sems.at[1]),
@@ -264,15 +304,31 @@
             second_pair(pair, rows, sides[1 - h], (slices_a[1 - h], slices_b[1 - h]))
         return carry
 
+    fetch.wait()
     lax.fori_loop(0, (PAIRS + 2) // 2, step, 0)
-    lax.fori_loop(0, PARTICLES, insert_late, 0)
-
-    def finish(i, carry):
-        rows = pl.ds(pl.multiple_of(i * 512, 512), 512)
-        out_ref[rows, :] = table[rows, :].astype(jnp.bfloat16)
-        return carry
-
-    lax.fori_loop(0, 2 * CELLS // 512, finish, 0)
+    for block in range(PARTICLES // 16):
+        @pl.when(span_s[4, 16 * block] > 0)
+        def _():
+            lax.fori_loop(16 * block, 16 * block + 16, insert_late, 0)
+
+
+    def leave(c):
+        return pltpu.make_async_copy(
+            staged.at[c % 2], out_ref.at[pl.ds(c * CHUNK, CHUNK)], sems.at[c % 2])
+
+    for c in range(2 * CELLS // CHUNK):
+        if c >= 2:
+            leave(c - 2).wait()
+
+        def convert(i, carry):
+            rows = pl.ds(pl.multiple_of(i * 512, 512), 512)
+            staged[c % 2, rows, :] = table[pl.ds(pl.multiple_of(c * CHUNK + i * 512, 512), 512), :].astype(jnp.bfloat16)
+            return carry
+
+        lax.fori_loop(0, CHUNK // 512, convert, 0)
+        leave(c).start()
+    for c in range(2 * CELLS // CHUNK - 2, 2 * CELLS // CHUNK):
+        leave(c).wait()
 
 
 def insert(patches, places, stacked, mixed, factors):
@@ -280,8 +336,8 @@
     return pl.pallas_call(
         insert_kernel,
         out_shape=jax.ShapeDtypeStruct((2 * CELLS, BOX), jnp.bfloat16),
-        in_specs=[whole] * 8,
-        out_specs=whole,
+        in_specs=[pl.BlockSpec(memory_space=pltpu.HBM)] + [whole] * 7,
+        out_specs=pl.BlockSpec(memory_space=pltpu.HBM),
         scratch_shapes=[
             pltpu.VMEM((3, SLOTS, 2 * BOX), jnp.int32),
             pltpu.VMEM((8, BOX), jnp.int32),
@@ -294,11 +350,13 @@
             [pltpu.VMEM((2 * BOX, 2 * BOX), jnp.bfloat16)] * 2,
             [pltpu.VMEM((2 * BOX, BOX), jnp.float32)] * 2,
             [pltpu.VMEM((2 * BOX, BOX), jnp.float32)] * 2,
+            pltpu.VMEM((2, CHUNK, BOX), jnp.bfloat16),
             pltpu.VMEM((PARTICLES, 2 * BOX, BOX), jnp.float32),
             pltpu.VMEM((2 * CELLS + 4 * GROUP, BOX), jnp.float32),
-            pltpu.SemaphoreType.DMA((5,)),
+            pltpu.VMEM((PAIRS, BOX, 2 * BOX), jnp.bfloat16),
+            pltpu.SemaphoreType.DMA((6,)),
         ],
-        compiler_params=pltpu.CompilerParams(vmem_limit_bytes=46 * 2**20),
+        compiler_params=pltpu.CompilerParams(vmem_limit_bytes=62 * 2**20),
         name="insert_slices",
     )(patches, places, stacked, mixed, *factors)
 
@@ -500,7 +558,7 @@
             dma((2, XS - 1)), dma((2, XS - 1)), dma((2, ZS - 1)), dma((2, ZS - 1)),
         ],
         compiler_params=pltpu.CompilerParams(
-            collective_id=0, has_side_effects=True, vmem_limit_bytes=60 * 2**20),
+            collective_id=0, has_side_effects=True, vmem_limit_bytes=57 * 2**20),
         name="reduce_table",
     )(table)
 
@@ -525,9 +583,8 @@
 
 
 def body(tilt_images, corners, visible, defocus, labels, row_owner, row_offset):
-    misc = jnp.stack([defocus.reshape(BOX), jnp.repeat(labels.astype(jnp.float32), TILTS)])
     patches, places, *factors = swap(
-        corners[:, 0], visible, tilt_images[0], row_owner[..., 0], row_offset, misc)
+        corners[:, 0], visible, tilt_images[0], row_owner[..., 0], row_offset, defocus, labels[None])
     stacked, mixed = tables()
     return reduce_table(insert(patches, places, stacked, mixed, factors))
 

time: 111 us -> 105 us (0.946)
  local copies, waits for them, and re-layouts: 6.5 us -> 1.67 us
  Pallas kernels: 102 us -> 100 us
    unnamed x11 -> x1, local copies, waits for them, and re-layouts: 5.58 us -> 1.67 us
    pallas_call x1, Pallas kernels: 26.3 us -> 23.5 us  [swap(): pl.pallas_call(swap_kernel, out_shape=[jax.ShapeDtypeStruct((PAIRS, BOX,...]
    pallas_call x1, Pallas kernels: 37.3 us -> 38.5 us  [insert(): pl.pallas_call(insert_kernel, out_shape=jax.ShapeDtypeStruct((2 * CELLS,...]
where the time goes in v5:
time: 105 us; the launch traced here: 104 us
  Pallas kernels  100 us (95%)
  other arithmetic  2.13 us (2%)
  local copies, waits for them, and re-layouts  1.67 us (2%)
    pallas_call x1, Pallas kernels, insert(): pl.pallas_call(insert_kernel, out_shape=jax.ShapeDtypeStruct((2 * CELLS,...  38.5 us
    pallas_call x1, Pallas kernels, reduce_table(): pl.pallas_call(reduce_kernel, out_shape=jax.ShapeDtypeStruct((2, HALFMAPS...  38.2 us
    pallas_call x1, Pallas kernels, swap(): pl.pallas_call(swap_kernel, out_shape=[jax.ShapeDtypeStruct((PAIRS, BOX,...  23.5 us

profile of v5, /device:TPU:8, one launch (start us, length us, event | category | flops | bytes accessed | tf_op | source)
XLA Modules:
  0.0 104.2 jit_solution(8963624776784680453)
XLA Ops:
  0.0 0.3 fusion.12
  0.3 0.6 negate_convert_fusion
  0.8 0.7 maximum_maximum_fusion.mixed_ref
  1.5 0.6 pad_maximum_fusion.stacked_ref
  2.1 23.5 %swap_rows.1 = (bf16[64,128,256]{2,1,0:T(8,128)(2,1)}, s32[128,128]{1,0:T(8,128)}, f32[128,128]{1,0:T(8,128)}, f32[128,128]{1,0:T(8,128)}, f32[128,128]{1,0:T(8,128)}, /*index=5*/f32[128,128]{1,0:T(8,128)}) custom-call(s32[2,128]{1,0:T(2,128)} %bitcast.6, s32[1,128]{1,0:T(1,128)} %seen_hbm.1, bf16[256,256]{1,0:T(8,128)(2,1)} %bitcast.4, ...), custom_call_target="tpu_custom_call" | custom-call | tf_op jit(solution)/shard_map/swap_rows/pallas_call | solution.py:150
  25.7 38.5 %insert_slices.1.table_ref = bf16[32768,128]{1,0:T(8,128)(2,1)} custom-call(bf16[64,128,256]{2,1,0:T(8,128)(2,1)} %get-tuple-element.11.patches_hbm, s32[128,128]{1,0:T(8,128)} %get-tuple-element.12.places_ref, bf16[256,128]{1,0:T(8,128)(2,1)} %pad_maximum_fusion.stacked_ref, bf16[256,256]{1,0:T(8,128)(2,1)} %maximum_maximum_fusion.mixed_ref, ...), custom_call_target="tpu_custom_call" | custom-call | tf_op jit(solution)/shard_map/insert_slices/pallas_call | solution.py:336
  64.2 38.2 %reduce_table.1 = f32[2,4,64,128]{3,2,1,0:T(8,128)} custom-call(bf16[32768,128]{1,0:T(8,128)(2,1)} %insert_slices.1.table_ref), custom_call_target="tpu_custom_call" | custom-call | tf_op jit(solution)/shard_map/reduce_table/pallas_call | solution.py:537
  102.5 1.7 %copy.9 = f32[2,4,64,128]{3,2,1,0:T(8,128)} copy(f32[2,4,64,128]{3,2,1,0:T(8,128)} %reduce_table.1) | data formatting | bytes 524288
  (1 shorter events, 0.0 us)

commit v6 on v5

--- a/solution.py
+++ b/solution.py
@@ -14,10 +14,10 @@
 TILTS = 64
 PARTICLES = 128
 CELLS = TILTS * HALFMAPS * 64
-GROUP = 8
+GROUP = 4
 PAIRS = PARTICLES // 2
 WINDOW = 2 * GROUP
-SLOTS = 64
+SLOTS = 104
 CUTS = 8
 CHUNK = 4096
 
@@ -178,50 +178,46 @@
 
 
 def insert_kernel(patches_hbm, places_ref, stacked_ref, mixed_ref, first_ref, second_ref, cos_ref, sin_ref, out_ref,
-                  lists, spans, late_rows, spot_s, row_s, late_s, span_s, late_rows_s, sides, slices_a, slices_b, staged, kept_slices, table, patches_ref, sems):
+                  lists, spans, late_rows, spot_s, row_s, late_s, span_s, late_rows_s, sides, slices, staged, kept_slices, table, patches_ref, sems):
     fetch = pltpu.make_async_copy(patches_hbm, patches_ref, sems.at[5])
     fetch.start()
     entry = lax.broadcasted_iota(jnp.int32, (8, BOX), 0)
+    lane = lax.broadcasted_iota(jnp.int32, (8, BOX), 1)
     rank = jnp.zeros((8, BOX), jnp.int32)
     spots = [2 * CELLS + 2 * ((8 * s + entry) % (2 * GROUP)) for s in range(SLOTS // 8)]
     spare = jnp.concatenate(spots, axis=0)
     sources = [jnp.zeros((8, BOX), jnp.int32) for _ in range(SLOTS // 8)]
-    first_row, last_row = jnp.full((8, BOX), BOX, jnp.int32), jnp.zeros((8, BOX), jnp.int32)
-    for j in range(BOX // 8):
-        place = places_ref[8 * j:8 * j + 8, :]
-        kept = place >= 0
-        for s in range(SLOTS // 8):
-            hit = kept & (rank == s)
-            spots[s] = jnp.where(hit, place, spots[s])
-            sources[s] = jnp.where(hit, 2 * (8 * j + entry), sources[s])
-        over = kept & (rank >= SLOTS // 8)
-        late_rows[8 * j:8 * j + 8, :] = jnp.where(over, place, 2 * CELLS)
-        first_row = jnp.minimum(first_row, jnp.where(over, 8 * j + entry, BOX))
-        last_row = jnp.maximum(last_row, jnp.where(over, 8 * j + entry + 1, 0))
-        rank = rank + jnp.where(kept, 1, 0)
+    bounds = []
+    for j in range(2):
+        first_row, last_row = jnp.full((8, BOX), BOX, jnp.int32), jnp.zeros((8, BOX), jnp.int32)
+        for block in range(BOX // 8):
+            place = places_ref[8 * block:8 * block + 8, :]
+            if j == 1:
+                place = pltpu.roll(place, PAIRS, axis=1)
+            kept = (place >= 0) & (lane < PAIRS)
+            for s in range(SLOTS // 8):
+                hit = kept & (rank == s)
+                spots[s] = jnp.where(hit, place, spots[s])
+                sources[s] = jnp.where(hit, 2 * (BOX * j + 8 * block + entry), sources[s])
+            over = kept & (rank >= SLOTS // 8)
+            late_rows[j, 8 * block:8 * block + 8, :] = jnp.where(over, place, 2 * CELLS)
+            first_row = jnp.minimum(first_row, jnp.where(over, 8 * block + entry, BOX))
+            last_row = jnp.maximum(last_row, jnp.where(over, 8 * block + entry + 1, 0))
+            rank = rank + jnp.where(kept, 1, 0)
+        bounds += [jnp.min(first_row, axis=0, keepdims=True), jnp.max(last_row, axis=0, keepdims=True)]
     spot = jnp.concatenate(spots, axis=0)
     slot = lax.broadcasted_iota(jnp.int32, (SLOTS, BOX), 0)
     late = jnp.zeros((SLOTS, BOX), jnp.bool_)
     for d in range(1, WINDOW):
         late = late | ((pltpu.roll(spot, SLOTS - d, axis=0) == spot) & (slot < SLOTS - d))
-    lists[0, :, :BOX] = jnp.where(late, spare, spot)
-    lists[0, :, BOX:] = spare
-    lists[1, :, :BOX] = jnp.concatenate(sources, axis=0)
-    lists[1, :, BOX:] = jnp.zeros((SLOTS, BOX), jnp.int32)
-    lists[2, :, :BOX] = jnp.where(late, spot, spare)
-    lists[2, :, BOX:] = spare
-    row = lax.broadcasted_iota(jnp.int32, (8, BOX), 0)
-    bounds = [
-        jnp.min(jnp.where(late, slot, SLOTS), axis=0, keepdims=True),
-        jnp.max(jnp.where(late, slot + 1, 0), axis=0, keepdims=True),
-        jnp.min(first_row, axis=0, keepdims=True),
-        jnp.max(last_row, axis=0, keepdims=True),
-    ]
-    spans[...] = jnp.where(row == 0, bounds[0], jnp.where(row == 1, bounds[1], jnp.where(row == 2, bounds[2], bounds[3])))
-    amount = bounds[1] + bounds[3]
-    for shift in (1, 2, 4, 8):
-        amount = amount + pltpu.roll(amount, BOX - shift, axis=1)
-    spans[4:5, :] = amount
+    lists[0] = jnp.where(late, spare, spot)
+    lists[1] = jnp.concatenate(sources, axis=0)
+    lists[2] = jnp.where(late, spot, spare)
+    bounds += [jnp.min(jnp.where(late, slot, SLOTS), axis=0, keepdims=True),
+               jnp.max(jnp.where(late, slot + 1, 0), axis=0, keepdims=True)]
+    for i, bound in enumerate(bounds):
+        spans[i:i + 1, :] = bound
+    spans[6:7, :] = bounds[1] + bounds[3] + bounds[5]
     copies = [
         pltpu.make_async_copy(lists.at[0], spot_s, sems.at[0]),
         pltpu.make_async_copy(lists.at[1], row_s, sems.at[1]),
@@ -237,7 +233,7 @@
         return carry
 
     lax.fori_loop(0, 2 * CELLS // 512, clear, 0)
-    for copy in copies:
+    for copy in copies[:2]:
         copy.wait()
 
     def line(pair, j):
@@ -249,19 +245,19 @@
             target[j * BOX:(j + 1) * BOX, :BOX] = section[:BOX, j * BOX:(j + 1) * BOX]
             target[j * BOX:(j + 1) * BOX, BOX:] = section[BOX:, j * BOX:(j + 1) * BOX]
 
-    def second_pair(pair, rows, source, targets):
+    def second_pair(pair, rows, source, target):
         spectrum = jnp.dot(source[...], mixed_ref[...], preferred_element_type=jnp.float32)
-        for j, target in enumerate(targets):
+        for j in range(2):
             pick = jnp.full((BOX, BOX), line(pair, j), jnp.int32)
             first = jnp.take_along_axis(first_ref[...], pick, axis=1)
             second = jnp.take_along_axis(second_ref[...], pick, axis=1)
             transfer = first * rows[j][0] + second * rows[j][1]
             real = transfer * spectrum[j * BOX:(j + 1) * BOX, :BOX]
             imag = transfer * spectrum[j * BOX:(j + 1) * BOX, BOX:]
-            target[pl.ds(0, BOX, stride=2), :] = real
-            target[pl.ds(1, BOX, stride=2), :] = imag
-            kept_slices[line(pair, j), pl.ds(0, BOX, stride=2), :] = real
-            kept_slices[line(pair, j), pl.ds(1, BOX, stride=2), :] = imag
+            target[pl.ds(2 * BOX * j, BOX, stride=2), :] = real
+            target[pl.ds(2 * BOX * j + 1, BOX, stride=2), :] = imag
+            kept_slices[pair, pl.ds(2 * BOX * j, BOX, stride=2), :] = real
+            kept_slices[pair, pl.ds(2 * BOX * j + 1, BOX, stride=2), :] = imag
 
     def insert(p, source):
         waiting = None
@@ -276,18 +272,19 @@
             waiting = (spots, sums)
 
     def insert_late(p, carry):
-        @pl.when(span_s[1, p] + span_s[3, p] > 0)
+        @pl.when(span_s[6, p] > 0)
         def _():
             def from_slot(i, carry):
                 table[pl.ds(late_s[i, p], 2), :] += kept_slices[p, pl.ds(row_s[i, p], 2), :]
                 return carry
 
-            def from_row(i, carry):
-                table[pl.ds(late_rows_s[i, p], 2), :] += kept_slices[p, pl.ds(2 * i, 2), :]
-                return carry
-
-            lax.fori_loop(span_s[0, p], span_s[1, p], from_slot, 0)
-            lax.fori_loop(span_s[2, p], span_s[3, p], from_row, 0)
+            lax.fori_loop(span_s[4, p], span_s[5, p], from_slot, 0)
+            for j in range(2):
+                def from_row(i, carry):
+                    table[pl.ds(late_rows_s[j, i, p], 2), :] += kept_slices[p, pl.ds(2 * BOX * j + 2 * i, 2), :]
+                    return carry
+
+                lax.fori_loop(span_s[2 * j, p], span_s[2 * j + 1, p], from_row, 0)
 
         return carry
 
@@ -298,19 +295,16 @@
             pair = jnp.clip(tick - 1, 0, PAIRS - 1)
             rows = [(cos_ref[pl.ds(line(pair, j), 1), :], sin_ref[pl.ds(line(pair, j), 1), :]) for j in range(2)]
             idle = (tick < 2) | (tick >= PAIRS + 2)
-            insert(jnp.where(idle, PARTICLES, tick - 2), slices_a[h])
-            insert(jnp.where(idle, PARTICLES, line(tick - 2, 1)), slices_b[h])
+            insert(jnp.where(idle, PAIRS, tick - 2), slices[h])
             first_pair(patch, sides[h])
-            second_pair(pair, rows, sides[1 - h], (slices_a[1 - h], slices_b[1 - h]))
+            second_pair(pair, rows, sides[1 - h], slices[1 - h])
         return carry
 
     fetch.wait()
     lax.fori_loop(0, (PAIRS + 2) // 2, step, 0)
-    for block in range(PARTICLES // 16):
-        @pl.when(span_s[4, 16 * block] > 0)
-        def _():
-            lax.fori_loop(16 * block, 16 * block + 16, insert_late, 0)
-
+    for copy in copies[2:]:
+        copy.wait()
+    lax.fori_loop(0, PAIRS, insert_late, 0)
 
     def leave(c):
         return pltpu.make_async_copy(
@@ -339,19 +333,18 @@
         in_specs=[pl.BlockSpec(memory_space=pltpu.HBM)] + [whole] * 7,
         out_specs=pl.BlockSpec(memory_space=pltpu.HBM),
         scratch_shapes=[
-            pltpu.VMEM((3, SLOTS, 2 * BOX), jnp.int32),
+            pltpu.VMEM((3, SLOTS, BOX), jnp.int32),
             pltpu.VMEM((8, BOX), jnp.int32),
-            pltpu.VMEM((BOX, BOX), jnp.int32),
-            pltpu.SMEM((SLOTS, 2 * BOX), jnp.int32),
-            pltpu.SMEM((SLOTS, 2 * BOX), jnp.int32),
-            pltpu.SMEM((SLOTS, 2 * BOX), jnp.int32),
+            pltpu.VMEM((2, BOX, BOX), jnp.int32),
+            pltpu.SMEM((SLOTS, BOX), jnp.int32),
+            pltpu.SMEM((SLOTS, BOX), jnp.int32),
+            pltpu.SMEM((SLOTS, BOX), jnp.int32),
             pltpu.SMEM((8, BOX), jnp.int32),
-            pltpu.SMEM((BOX, BOX), jnp.int32),
+            pltpu.SMEM((2, BOX, BOX), jnp.int32),
             [pltpu.VMEM((2 * BOX, 2 * BOX), jnp.bfloat16)] * 2,
-            [pltpu.VMEM((2 * BOX, BOX), jnp.float32)] * 2,
-            [pltpu.VMEM((2 * BOX, BOX), jnp.float32)] * 2,
+            [pltpu.VMEM((4 * BOX, BOX), jnp.float32)] * 2,
             pltpu.VMEM((2, CHUNK, BOX), jnp.bfloat16),
-            pltpu.VMEM((PARTICLES, 2 * BOX, BOX), jnp.float32),
+            pltpu.VMEM((PAIRS, 4 * BOX, BOX), jnp.float32),
             pltpu.VMEM((2 * CELLS + 4 * GROUP, BOX), jnp.float32),
             pltpu.VMEM((PAIRS, BOX, 2 * BOX), jnp.bfloat16),
             pltpu.SemaphoreType.DMA((6,)),

time: 105 us -> 97.3 us (0.927)
  Pallas kernels: 100 us -> 92.7 us
    pallas_call x1, Pallas kernels: 38.5 us -> 31 us  [insert(): pl.pallas_call(insert_kernel, out_shape=jax.ShapeDtypeStruct((2 * CELLS,...]
where the time goes in v6:
time: 97.3 us; the launch traced here: 96.5 us
  Pallas kernels  92.7 us (95%)
  other arithmetic  2.13 us (2%)
  local copies, waits for them, and re-layouts  1.67 us (2%)
    pallas_call x1, Pallas kernels, reduce_table(): pl.pallas_call(reduce_kernel, out_shape=jax.ShapeDtypeStruct((2, HALFMAPS...  38.2 us
    pallas_call x1, Pallas kernels, insert(): pl.pallas_call(insert_kernel, out_shape=jax.ShapeDtypeStruct((2 * CELLS,...  31 us
    pallas_call x1, Pallas kernels, swap(): pl.pallas_call(swap_kernel, out_shape=[jax.ShapeDtypeStruct((PAIRS, BOX,...  23.5 us

profile of v6, /device:TPU:8, one launch (start us, length us, event | category | flops | bytes accessed | tf_op | source)
XLA Modules:
  0.0 96.5 jit_solution(10570764206938901324)
XLA Ops:
  0.0 0.3 fusion.12
  0.3 0.6 negate_convert_fusion
  0.8 0.7 maximum_maximum_fusion.mixed_ref
  1.5 0.6 pad_maximum_fusion.stacked_ref
  2.1 23.5 %swap_rows.1 = (bf16[64,128,256]{2,1,0:T(8,128)(2,1)}, s32[128,128]{1,0:T(8,128)}, f32[128,128]{1,0:T(8,128)}, f32[128,128]{1,0:T(8,128)}, f32[128,128]{1,0:T(8,128)}, /*index=5*/f32[128,128]{1,0:T(8,128)}) custom-call(s32[2,128]{1,0:T(2,128)} %bitcast.6, s32[1,128]{1,0:T(1,128)} %seen_hbm.1, bf16[256,256]{1,0:T(8,128)(2,1)} %bitcast.4, ...), custom_call_target="tpu_custom_call" | custom-call | tf_op jit(solution)/shard_map/swap_rows/pallas_call | solution.py:150
  25.7 31.0 %insert_slices.1.table_ref = bf16[32768,128]{1,0:T(8,128)(2,1)} custom-call(bf16[64,128,256]{2,1,0:T(8,128)(2,1)} %get-tuple-element.11.patches_hbm, s32[128,128]{1,0:T(8,128)} %get-tuple-element.12.places_ref, bf16[256,128]{1,0:T(8,128)(2,1)} %pad_maximum_fusion.stacked_ref, bf16[256,256]{1,0:T(8,128)(2,1)} %maximum_maximum_fusion.mixed_ref, ...), custom_call_target="tpu_custom_call" | custom-call | tf_op jit(solution)/shard_map/insert_slices/pallas_call | solution.py:330
  56.7 38.2 %reduce_table.1 = f32[2,4,64,128]{3,2,1,0:T(8,128)} custom-call(bf16[32768,128]{1,0:T(8,128)(2,1)} %insert_slices.1.table_ref), custom_call_target="tpu_custom_call" | custom-call | tf_op jit(solution)/shard_map/reduce_table/pallas_call | solution.py:530
  94.9 1.7 %copy.9 = f32[2,4,64,128]{3,2,1,0:T(8,128)} copy(f32[2,4,64,128]{3,2,1,0:T(8,128)} %reduce_table.1) | data formatting | bytes 524288
  (1 shorter events, 0.0 us)

commit v7 on v6

--- a/solution.py
+++ b/solution.py
@@ -42,7 +42,7 @@
 
 def swap_kernel(corner_hbm, seen_hbm, image_hbm, owner_hbm, offset_hbm, defocus_hbm, label_hbm, patches_hbm, places_ref,
                 first_ref, second_ref, cos_ref, sin_ref, corner_ref, seen_ref, image_ref, owner_ref, offset_ref,
-                defocus_ref, label_ref, left, right, outbox, inbox, patches_ref, send_sem, recv_sem, load_sem, store_sem):
+                defocus_ref, label_ref, left, right, rows_ref, outbox, between, inbox, patches_ref, send_sem, recv_sem, load_sem, store_sem):
     loads = [
         pltpu.make_async_copy(source, target, load_sem.at[i]) for i, (source, target) in enumerate((
             (owner_hbm, owner_ref), (offset_hbm, offset_ref), (defocus_hbm, defocus_ref), (label_hbm, label_ref),
@@ -52,34 +52,43 @@
     tilt, slab = lax.axis_index("tilt"), lax.axis_index("slab")
     barrier = pltpu.get_barrier_semaphore()
 
-    def peer(d):
-        return (tilt + d) % TILTS
-
-    def greet(d, carry):
-        pl.semaphore_signal(barrier, inc=1, device_id=(peer(d), slab), device_id_type=pl.DeviceIdType.MESH)
-        return carry
-
-    lax.fori_loop(1, TILTS, greet, 0)
+    z, side = tilt // 2 % ZS, tilt // (2 * ZS) * 2 + tilt % 2
+
+    def along_z(other):
+        return (tilt - 2 * z + 2 * other, slab)
+
+    def along_side(other):
+        return (other // 2 * (2 * ZS) + 2 * z + other % 2, slab)
+
+    for d in range(1, 8):
+        for partner in (along_z((z + d) % 8), along_side((side + d) % 8)):
+            pl.semaphore_signal(barrier, inc=1, device_id=partner, device_id_type=pl.DeviceIdType.MESH)
     for load in loads[:4]:
         load.wait()
     column = lax.broadcasted_iota(jnp.int32, (TILTS, BOX), 1)
     for j in range(2):
-        outbox[:, j, :] = (owner_ref[j] * 64 + offset_ref[j]).astype(jnp.float32)
-        outbox[:, 2, j * TILTS:(j + 1) * TILTS] = jnp.broadcast_to(defocus_ref[j:j + 1, :], (TILTS, TILTS))
-    outbox[:, 3, :] = jnp.where(column < TILTS, label_ref[0, 0], label_ref[0, 1]).astype(jnp.float32)
-    pl.semaphore_wait(barrier, TILTS - 1)
-
-    def message(to, origin):
+        rows_ref[j] = (owner_ref[j] * 64 + offset_ref[j]).astype(jnp.float32)
+        outbox[:, :, 2, j * TILTS:(j + 1) * TILTS] = jnp.broadcast_to(
+            defocus_ref[j:j + 1, :].reshape(1, 1, TILTS), (8, 8, TILTS))
+        for to in range(8):
+            outbox[:, to, j, :] = rows_ref[j, pl.ds(to // 2 * 16 + to % 2, 8, stride=2), :]
+    column = lax.broadcasted_iota(jnp.int32, (8, 8, BOX), 2)
+    outbox[:, :, 3, :] = jnp.where(column < TILTS, label_ref[0, 0], label_ref[0, 1]).astype(jnp.float32)
+    pl.semaphore_wait(barrier, 14)
+
+    def first_message(to, origin):
         return pltpu.make_async_remote_copy(
-            src_ref=outbox.at[to], dst_ref=inbox.at[origin], send_sem=send_sem.at[to], recv_sem=recv_sem.at[origin],
-            device_id=(to, slab), device_id_type=pl.DeviceIdType.MESH)
-
-    def send(d, carry):
-        message(peer(d), tilt).start()
-        return carry
-
-    lax.fori_loop(1, TILTS, send, 0)
-    inbox[tilt] = outbox[tilt]
+            src_ref=outbox.at[to], dst_ref=between.at[origin], send_sem=send_sem.at[0, to],
+            recv_sem=recv_sem.at[0, origin], device_id=along_z(to), device_id_type=pl.DeviceIdType.MESH)
+
+    def second_message(to, origin):
+        return pltpu.make_async_remote_copy(
+            src_ref=between.at[:, to], dst_ref=inbox.at[origin], send_sem=send_sem.at[1, to],
+            recv_sem=recv_sem.at[1, origin], device_id=along_side(to), device_id_type=pl.DeviceIdType.MESH)
+
+    for d in range(1, 8):
+        first_message((z + d) % 8, z).start()
+    between[z] = outbox[z]
     for load in loads[4:]:
         load.wait()
     left[...] = image_ref[:, :BOX].astype(jnp.float32)
@@ -103,26 +112,35 @@
         return pltpu.make_async_copy(patches_ref.at[pairs], patches_hbm.at[pairs], store_sem.at[i])
 
     def cut_pairs(i, carry):
-        windows = [window(CUTS * i + j) for j in range(CUTS)]
+        windows = []
+        for j in range(CUTS):
+            pair = CUTS // 2 * i + j // 2
+            source = pair // 16 * 16 + pair % 8 * 2 + pair // 8 % 2
+            windows.append(window(2 * source + j % 2))
         for j, patch in enumerate(windows):
             patches_ref[CUTS // 2 * i + j // 2, :, j % 2 * BOX:(j % 2 + 1) * BOX] = patch
         leave(i).start()
         return carry
 
-    lax.fori_loop(0, PARTICLES // CUTS, cut_pairs, 0)
-
-    def receive(d, carry):
-        message(tilt, peer(d)).wait_recv()
-        return carry
-
-    lax.fori_loop(1, TILTS, receive, 0)
-
-    rows = jnp.concatenate([inbox[:, 0, :], inbox[:, 1, :]], axis=0).astype(jnp.int32)
-    misc = jnp.concatenate([inbox[:, 2, :]] * 2, axis=0)
+    lax.fori_loop(0, PARTICLES // CUTS // 2, cut_pairs, 0)
+    for d in range(1, 8):
+        first_message(z, (z + d) % 8).wait_recv()
+    for d in range(1, 8):
+        second_message((side + d) % 8, side).start()
+    inbox[side] = between[:, side]
+    lax.fori_loop(PARTICLES // CUTS // 2, PARTICLES // CUTS, cut_pairs, 0)
+    for d in range(1, 8):
+        second_message(side, (side + d) % 8).wait_recv()
+
+    def received(r):
+        return inbox[:, :, r, :].reshape(TILTS, BOX)
+
+    rows = jnp.concatenate([received(0), received(1)], axis=0).astype(jnp.int32)
+    misc = jnp.concatenate([received(2)] * 2, axis=0)
     line = lax.broadcasted_iota(jnp.int32, (BOX, BOX), 0)
     mine = jnp.where(lane == jnp.where(line < TILTS, tilt, TILTS + tilt), misc, 0.0)
     defocus = jnp.sum(mine, axis=1, keepdims=True)
-    labels = jnp.concatenate([inbox[:, 3, :]] * 2, axis=0)
+    labels = jnp.concatenate([received(3)] * 2, axis=0)
     label = jnp.sum(jnp.where(lane == jnp.where(line < TILTS, 0, TILTS), labels, 0.0), axis=1, keepdims=True)
     places_ref[...] = places_of(rows, label.astype(jnp.int32), slab, lax.axis_size("slab")).T
     first, second, cos_part, sin_part = transfer_factors(defocus, lane)
@@ -131,11 +149,9 @@
     cos_ref[...] = cos_part
     sin_ref[...] = sin_part
 
-    def sent(d, carry):
-        message(peer(d), tilt).wait_send()
-        return carry
-
-    lax.fori_loop(1, TILTS, sent, 0)
+    for d in range(1, 8):
+        first_message((z + d) % 8, z).wait_send()
+        second_message((side + d) % 8, side).wait_send()
 
     def left_all(i, carry):
         leave(i).wait()
@@ -163,11 +179,13 @@
             pltpu.SMEM((1, 2), jnp.int32),
             pltpu.VMEM((256, BOX), jnp.float32),
             pltpu.VMEM((256, BOX), jnp.float32),
-            pltpu.VMEM((TILTS, 4, BOX), jnp.float32),
-            pltpu.VMEM((TILTS, 4, BOX), jnp.float32),
+            pltpu.VMEM((2, TILTS, BOX), jnp.float32),
+            pltpu.VMEM((8, 8, 4, BOX), jnp.float32),
+            pltpu.VMEM((8, 8, 4, BOX), jnp.float32),
+            pltpu.VMEM((8, 8, 4, BOX), jnp.float32),
             pltpu.VMEM((PAIRS, BOX, 2 * BOX), jnp.bfloat16),
-            pltpu.SemaphoreType.DMA((TILTS,)),
-            pltpu.SemaphoreType.DMA((TILTS,)),
+            pltpu.SemaphoreType.DMA((2, 8)),
+            pltpu.SemaphoreType.DMA((2, 8)),
             pltpu.SemaphoreType.DMA((7,)),
             pltpu.SemaphoreType.DMA((PARTICLES // CUTS,)),
         ],

time: 97.3 us -> 95.9 us (0.986)
    pallas_call x1, Pallas kernels: 23.5 us -> 20 us  [swap(): pl.pallas_call(swap_kernel, out_shape=[jax.ShapeDtypeStruct((PAIRS, BOX,...]
    pallas_call x1, Pallas kernels: 38.2 us -> 40.8 us  [reduce_table(): pl.pallas_call(reduce_kernel, out_shape=jax.ShapeDtypeStruct((2, HALFMAPS...]
where the time goes in v7:
time: 95.9 us; the launch traced here: 95.8 us
  Pallas kernels  91.9 us (96%)
  other arithmetic  2.13 us (2%)
  local copies, waits for them, and re-layouts  1.67 us (2%)
    pallas_call x1, Pallas kernels, reduce_table(): pl.pallas_call(reduce_kernel, out_shape=jax.ShapeDtypeStruct((2, HALFMAPS...  40.8 us
    pallas_call x1, Pallas kernels, insert(): pl.pallas_call(insert_kernel, out_shape=jax.ShapeDtypeStruct((2 * CELLS,...  31.2 us
    pallas_call x1, Pallas kernels, swap(): pl.pallas_call(swap_kernel, out_shape=[jax.ShapeDtypeStruct((PAIRS, BOX,...  20 us

profile of v7, /device:TPU:8, one launch (start us, length us, event | category | flops | bytes accessed | tf_op | source)
XLA Modules:
  0.0 95.8 jit_solution(7344352561462212364)
XLA Ops:
  0.0 0.3 fusion.12
  0.3 0.6 negate_convert_fusion
  0.8 0.7 maximum_maximum_fusion.mixed_ref
  1.5 0.6 pad_maximum_fusion.stacked_ref
  2.1 20.0 %swap_rows.1 = (bf16[64,128,256]{2,1,0:T(8,128)(2,1)}, s32[128,128]{1,0:T(8,128)}, f32[128,128]{1,0:T(8,128)}, f32[128,128]{1,0:T(8,128)}, f32[128,128]{1,0:T(8,128)}, /*index=5*/f32[128,128]{1,0:T(8,128)}) custom-call(s32[2,128]{1,0:T(2,128)} %bitcast.6, s32[1,128]{1,0:T(1,128)} %seen_hbm.1, bf16[256,256]{1,0:T(8,128)(2,1)} %bitcast.4, ...), custom_call_target="tpu_custom_call" | custom-call | tf_op jit(solution)/shard_map/swap_rows/pallas_call | solution.py:166
  22.1 31.2 %insert_slices.1.table_ref = bf16[32768,128]{1,0:T(8,128)(2,1)} custom-call(bf16[64,128,256]{2,1,0:T(8,128)(2,1)} %get-tuple-element.11.patches_hbm, s32[128,128]{1,0:T(8,128)} %get-tuple-element.12.places_ref, bf16[256,128]{1,0:T(8,128)(2,1)} %pad_maximum_fusion.stacked_ref, bf16[256,256]{1,0:T(8,128)(2,1)} %maximum_maximum_fusion.mixed_ref, ...), custom_call_target="tpu_custom_call" | custom-call | tf_op jit(solution)/shard_map/insert_slices/pallas_call | solution.py:348
  53.3 40.8 %reduce_table.1 = f32[2,4,64,128]{3,2,1,0:T(8,128)} custom-call(bf16[32768,128]{1,0:T(8,128)(2,1)} %insert_slices.1.table_ref), custom_call_target="tpu_custom_call" | custom-call | tf_op jit(solution)/shard_map/reduce_table/pallas_call | solution.py:548
  94.1 1.7 %copy.9 = f32[2,4,64,128]{3,2,1,0:T(8,128)} copy(f32[2,4,64,128]{3,2,1,0:T(8,128)} %reduce_table.1) | data formatting | bytes 524288
  (1 shorter events, 0.0 us)

commit v8 on v7

--- a/solution.py
+++ b/solution.py
@@ -22,12 +22,9 @@
 CHUNK = 4096
 
 
-def fourier_tables(width):
-    positions = jnp.arange(width, dtype=jnp.int32)
-    frequency = positions - width // 2
-    phase_index = frequency[:, None] * positions[None, :] % width
-    angles = phase_index.astype(jnp.float32) * (2.0 * jnp.pi / width)
-    return (jnp.cos(angles).astype(jnp.bfloat16), (-jnp.sin(angles)).astype(jnp.bfloat16))
+def fourier_tables(row, column):
+    angles = (((row - BOX // 2) * column) & (BOX - 1)).astype(jnp.float32) * (2.0 * math.pi / BOX)
+    return jnp.cos(angles), -jnp.sin(angles)
 
 
 def transfer_factors(defocus, column):
@@ -195,8 +192,8 @@
     )(*operands)
 
 
-def insert_kernel(patches_hbm, places_ref, stacked_ref, mixed_ref, first_ref, second_ref, cos_ref, sin_ref, out_ref,
-                  lists, spans, late_rows, spot_s, row_s, late_s, span_s, late_rows_s, sides, slices, staged, kept_slices, table, patches_ref, sems):
+def insert_kernel(patches_hbm, places_ref, first_ref, second_ref, cos_ref, sin_ref, out_ref,
+                  lists, spans, late_rows, spot_s, row_s, late_s, span_s, late_rows_s, sides, slices, staged, kept_slices, table, patches_ref, stacked_ref, mixed_ref, sems):
     fetch = pltpu.make_async_copy(patches_hbm, patches_ref, sems.at[5])
     fetch.start()
     entry = lax.broadcasted_iota(jnp.int32, (8, BOX), 0)
@@ -246,6 +243,15 @@
     for copy in copies:
         copy.start()
 
+    cos_table, sin_table = fourier_tables(
+        lax.broadcasted_iota(jnp.int32, (BOX, BOX), 0), lax.broadcasted_iota(jnp.int32, (BOX, BOX), 1))
+    stacked_ref[:BOX, :] = cos_table.astype(jnp.bfloat16)
+    stacked_ref[BOX:, :] = sin_table.astype(jnp.bfloat16)
+    mixed_ref[:BOX, :BOX] = cos_table.T.astype(jnp.bfloat16)
+    mixed_ref[:BOX, BOX:] = sin_table.T.astype(jnp.bfloat16)
+    mixed_ref[BOX:, :BOX] = (-sin_table).T.astype(jnp.bfloat16)
+    mixed_ref[BOX:, BOX:] = cos_table.T.astype(jnp.bfloat16)
+
     def clear(i, carry):
         table[pl.ds(pl.multiple_of(i * 512, 512), 512), :] = jnp.zeros((512, BOX), jnp.float32)
         return carry
@@ -343,12 +349,12 @@
         leave(c).wait()
 
 
-def insert(patches, places, stacked, mixed, factors):
+def insert(patches, places, factors):
     whole = pl.BlockSpec(memory_space=pltpu.VMEM)
     return pl.pallas_call(
         insert_kernel,
         out_shape=jax.ShapeDtypeStruct((2 * CELLS, BOX), jnp.bfloat16),
-        in_specs=[pl.BlockSpec(memory_space=pltpu.HBM)] + [whole] * 7,
+        in_specs=[pl.BlockSpec(memory_space=pltpu.HBM)] + [whole] * 5,
         out_specs=pl.BlockSpec(memory_space=pltpu.HBM),
         scratch_shapes=[
             pltpu.VMEM((3, SLOTS, BOX), jnp.int32),
@@ -365,11 +371,13 @@
             pltpu.VMEM((PAIRS, 4 * BOX, BOX), jnp.float32),
             pltpu.VMEM((2 * CELLS + 4 * GROUP, BOX), jnp.float32),
             pltpu.VMEM((PAIRS, BOX, 2 * BOX), jnp.bfloat16),
+            pltpu.VMEM((2 * BOX, BOX), jnp.bfloat16),
+            pltpu.VMEM((2 * BOX, 2 * BOX), jnp.bfloat16),
             pltpu.SemaphoreType.DMA((6,)),
         ],
         compiler_params=pltpu.CompilerParams(vmem_limit_bytes=62 * 2**20),
         name="insert_slices",
-    )(patches, places, stacked, mixed, *factors)
+    )(patches, places, *factors)
 
 
 ZS, XS = 8, 4
@@ -574,15 +582,6 @@
     )(table)
 
 
-def tables():
-    cos_table, sin_table = fourier_tables(BOX)
-    stacked = jnp.concatenate([cos_table, sin_table], 0)
-    mixed = jnp.concatenate([
-        jnp.concatenate([cos_table.T, sin_table.T], 1),
-        jnp.concatenate([-sin_table.T, cos_table.T], 1)], 0)
-    return stacked, mixed
-
-
 def places_of(rows, labels, slab_index, slab_count):
     owner, offset = rows // 64, rows % 64
     tilt = owner // slab_count
@@ -596,8 +595,7 @@
 def body(tilt_images, corners, visible, defocus, labels, row_owner, row_offset):
     patches, places, *factors = swap(
         corners[:, 0], visible, tilt_images[0], row_owner[..., 0], row_offset, defocus, labels[None])
-    stacked, mixed = tables()
-    return reduce_table(insert(patches, places, stacked, mixed, factors))
+    return reduce_table(insert(patches, places, factors))
 
 
 def solution(mesh):

time: 95.9 us -> 92.7 us (0.967); the launches traced: 95.8 us -> 91.5 us
  other arithmetic: 2.13 us -> 0 us
  Pallas kernels: 91.9 us -> 89.8 us
    pallas_call x1, Pallas kernels: 40.8 us -> 38.8 us  [reduce_table(): pl.pallas_call(reduce_kernel, out_shape=jax.ShapeDtypeStruct((2, HALFMAPS...]
    concatenate x2 -> x0, other arithmetic: 1.3 us -> none  [the longest x1 0.67 us: tables(): jnp.concatenate([jnp.concatenate([cos_table.T, sin_table.T], 1), jnp.conc...]
where the time goes in v8:
time: 92.7 us; the launch traced here: 91.5 us
  Pallas kernels  89.8 us (97%)
  local copies, waits for them, and re-layouts  1.67 us (2%)
    pallas_call x1, Pallas kernels, reduce_table(): pl.pallas_call(reduce_kernel, out_shape=jax.ShapeDtypeStruct((2, HALFMAPS...  38.8 us
    pallas_call x1, Pallas kernels, insert(): pl.pallas_call(insert_kernel, out_shape=jax.ShapeDtypeStruct((2 * CELLS,...  31 us
    pallas_call x1, Pallas kernels, swap(): pl.pallas_call(swap_kernel, out_shape=[jax.ShapeDtypeStruct((PAIRS, BOX,...  20 us

profile of v8, /device:TPU:8, one launch (start us, length us, event | category | flops | bytes accessed | tf_op | source)
XLA Modules:
  0.0 91.5 jit_solution(12612762904304619956)
XLA Ops:
  0.0 20.0 %swap_rows.1 = (bf16[64,128,256]{2,1,0:T(8,128)(2,1)}, s32[128,128]{1,0:T(8,128)}, f32[128,128]{1,0:T(8,128)}, f32[128,128]{1,0:T(8,128)}, f32[128,128]{1,0:T(8,128)}, /*index=5*/f32[128,128]{1,0:T(8,128)}) custom-call(s32[2,128]{1,0:T(2,128)} %bitcast.6, s32[1,128]{1,0:T(1,128)} %seen_hbm.1, bf16[256,256]{1,0:T(8,128)(2,1)} %bitcast.4, ...), custom_call_target="tpu_custom_call" | custom-call | tf_op jit(solution)/shard_map/swap_rows/pallas_call | solution.py:163
  20.1 31.0 %insert_slices.1.table_ref = bf16[32768,128]{1,0:T(8,128)(2,1)} custom-call(bf16[64,128,256]{2,1,0:T(8,128)(2,1)} %get-tuple-element.11.patches_hbm, s32[128,128]{1,0:T(8,128)} %get-tuple-element.12.places_ref, f32[128,128]{1,0:T(8,128)} %get-tuple-element.13.first_ref, f32[128,128]{1,0:T(8,128)} %get-tuple-element.14.second_ref, ...), custom_call_target="tpu_custom_call" | custom-call | tf_op jit(solution)/shard_map/insert_slices/pallas_call | solution.py:354
  51.0 38.8 %reduce_table.1 = f32[2,4,64,128]{3,2,1,0:T(8,128)} custom-call(bf16[32768,128]{1,0:T(8,128)(2,1)} %insert_slices.1.table_ref), custom_call_target="tpu_custom_call" | custom-call | tf_op jit(solution)/shard_map/reduce_table/pallas_call | solution.py:556
  89.9 1.7 %copy.9 = f32[2,4,64,128]{3,2,1,0:T(8,128)} copy(f32[2,4,64,128]{3,2,1,0:T(8,128)} %reduce_table.1) | data formatting | bytes 524288
